TPU v7x, 128 devices: a whole 4x4x4 slice. The times are simulated.
128 devices in a mesh: sub: 16 (over y, x), tm: 8 (over z, core).
Axes of the slice: x: 4, y: 4, z: 4, core: 2. Of those that a mesh axis runs over, the one named last changes fastest.
Arguments:
- voltages: bfloat16 [8192, 24, 2, 2048], P('sub', 'tm'), may hold values from -6 to 6
- slot_feed: int32 [2048], replicated, may hold values from 0 to 2047, each once
- chan_lag: int32 [8192], replicated, may hold values from 0 to 4096
- trial_dm: int32 [512], replicated, may hold values from 0 to 4096
- beam_order: int32 [1024], replicated, may hold values from 0 to 1023, each once
Outputs:
- dedispersed: float32 [1024, 24, 512], P('sub', 'tm')
Inputs may be any that keep to these rules, and one draw needn't show every extreme that they name: `slot_feed`: each feed once; slot (p * 4 + y) * 256 + n is polarization p at east-west position y and north-south position n. `beam_order`: each beam once.
All inputs are finite; a program needn't handle non-finite values.
Results may differ from a plain program's by a relative error of at most 0.00088.
Values may be sent and summed in bfloat16 or wider, within the bound.
A program may use at most 192 MiB of HBM per device.

v0:
```python
import math

import jax
import jax.numpy as jnp
from jax import lax
from jax.sharding import Mesh
from jax.sharding import PartitionSpec as P

NS = 256
CYL = 4
POL = 2
CHANNELS = 8192
NDM = 512
MAXD = 6
QUANT = 2796202
SUB = ("sub_0", "sub_1")


def shifted(value, axis, steps):
    count = lax.axis_size(axis)
    initial, last = (max(0, -steps), min(count, count - steps))
    return lax.ppermute(value, axis, [(source, source + steps) for source in range(initial, last)])


def summed_rows(total, axes):
    for axis in axes:
        total = lax.psum_scatter(total, axis, scatter_dimension=0, tiled=True)
    return total


def north_table():
    positions = jnp.arange(NS, dtype=jnp.int32)
    phase_index = positions[:, None] * positions[None, :] % NS
    angles = phase_index.astype(jnp.float32) * (2.0 * math.pi / NS)
    cosine = jnp.cos(angles) / math.sqrt(NS)
    sine_part = jnp.sin(angles) / math.sqrt(NS)
    real_row = jnp.stack([cosine, -sine_part], axis=1)
    imag_row = jnp.stack([sine_part, cosine], axis=1)
    return jnp.stack([real_row, imag_row], axis=0).astype(jnp.bfloat16)


def west_table():
    cylinder = jnp.arange(CYL, dtype=jnp.int32)
    quarter_turn = cylinder[:, None] * cylinder[None, :] % 4
    cosine = (quarter_turn == 0).astype(jnp.float32) - (quarter_turn == 2).astype(jnp.float32)
    sine_part = (quarter_turn == 1).astype(jnp.float32) - (quarter_turn == 3).astype(jnp.float32)
    real_row = jnp.stack([cosine, -sine_part], axis=2)
    imag_row = jnp.stack([sine_part, cosine], axis=2)
    return 0.5 * jnp.stack([real_row, imag_row], axis=1)


def compute_power(north_beams):
    west_beams = jnp.einsum(
        "ctpyom,yoeq->ctpeqm", north_beams, west_table(), precision=lax.Precision.HIGHEST
    )
    squares = jnp.sum(west_beams * west_beams, axis=(2, 4))
    return squares.reshape(north_beams.shape[0], north_beams.shape[1], CYL * NS)


def delay_table(lag_rows, trial_dm):
    return lag_rows[:, None] * trial_dm[None, :] // QUANT


def shift_sum(source, delays, head_rows, out_rows):
    time_rows = source.shape[1]
    total_sum = jnp.zeros((source.shape[2], out_rows, NDM), jnp.float32)
    for delay_step in range(MAXD + 1):
        onehot = (delays == delay_step).astype(jnp.bfloat16)
        first_index = head_rows - delay_step
        begin_row = max(0, first_index)
        end_row = min(time_rows, first_index + out_rows)
        window = source[:, begin_row:end_row, :]
        part = jnp.einsum("ctb,cd->btd", window, onehot, preferred_element_type=jnp.float32)
        total_sum = total_sum + part
    return total_sum


def per_device(voltages, slot_feed, chan_lag, trial_dm, beam_order):
    channel_count = voltages.shape[0]
    sample_count = voltages.shape[1]
    shard_reach = (MAXD + sample_count - 1) // sample_count
    grid_volts = jnp.take(voltages, slot_feed, axis=3).reshape(
        channel_count, sample_count, 2, POL, CYL, NS
    )
    north_beams = jnp.einsum(
        "ctrpyn,rnom->ctpyom", grid_volts, north_table(), preferred_element_type=jnp.float32
    )
    intensity = compute_power(north_beams)
    ordered = jnp.take(intensity, beam_order, axis=2)
    totals = lax.psum(jnp.sum(ordered, axis=1), "tm")
    average = totals / (sample_count * lax.axis_size("tm"))
    normal = (ordered - average[:, None, :]).astype(jnp.bfloat16)
    pieces = [normal]
    for distance in range(1, shard_reach + 1):
        earlier = shifted(normal, "tm", distance)
        pieces = [earlier] + pieces
    source = jnp.concatenate(pieces, axis=1)
    head_rows = MAXD
    offset = lax.axis_index(SUB) * channel_count
    lag_rows = lax.dynamic_slice_in_dim(chan_lag, offset, channel_count)
    delays = delay_table(lag_rows, trial_dm)
    result = summed_rows(shift_sum(source, delays, head_rows, sample_count), SUB)
    return result / math.sqrt(CHANNELS)


def solution(mesh):
    finer = Mesh(mesh.devices.reshape(4, 4, mesh.shape["tm"]), ("sub_0", "sub_1", "tm"))
    placed = (P(SUB, "tm", None, None), P(), P(), P(), P())
    return jax.shard_map(
        per_device, mesh=finer, in_specs=placed, out_specs=P(SUB, "tm", None), check_vma=False
    )
```

profile of v0, /device:TPU:1, one launch (start us, length us, event | category | flops | bytes accessed | tf_op | source)
XLA Modules:
  0.0 634.4 jit_solution(8743649440929038632)
XLA Ops:
  6.5 1.1 negate_convert_fusion
  7.6 1.0 fusion.61
  11.5 42.7 %copy.28 = bf16[512,3,2,2048]{0,1,2,3:T(4,128)(2,1)} copy(bf16[512,3,2,2048]{3,2,1,0:T(2,128)(2,1)} %param.5) | data formatting | bytes 25165824 | tf_op args[0]
  54.2 36.1 %gather_fusion = bf16[2048,512,3,2]{1,2,3,0:T(4,128)(2,1)} fusion(bf16[512,3,2,2048]{0,1,2,3:T(4,128)(2,1)} %copy.28, s32[2048]{0:T(1024)S(1)} %fusion.66), kind=kCustom, calls=%fused_computation | custom fusion | bytes 25174016 | tf_op jit(solution)/shard_map/jit(_take)/gather | solution.py:82
  90.3 24.9 %copy.29 = bf16[512,3,2,2,4,256]{5,0,2,4,3,1:T(8,128)(2,1)} copy(bf16[512,3,2,2,4,256]{0,1,2,5,4,3:T(4,128)(2,1)} %bitcast.85) | data formatting | bytes 25165824 | tf_op jit(solution)/shard_map/jit(_take)/gather | solution.py:82
  115.5 16.3 %fusion.8 = f32[512,3,2,4,2,256]{5,0,4,3,2,1:T(8,128)} fusion(bf16[512,3,2,2,4,256]{5,0,2,4,3,1:T(8,128)(2,1)} %copy.29, pred[2,4,256]{2,1,0:T(4,128)(4,1)S(1)} %broadcast_in_dim.34, bf16[1,256,2,256]{3,1,0,2:T(8,128)(2,1)S(1)} %get-tuple-element.6, bf16[1,256,2,256]{3,1,0,2:T(8,128)(2,1)S(1)} %get-tuple-element.5), kind=kOutput, calls=%fused_computation.11 | convolution fusion | flops 6449790976 | bytes 38275072 | tf_op jit(solution)/shard_map/ctrpyn,rnom->ctpyom/dot_general | solution.py:85
  131.8 88.4 %fusion = f32[4,512,3,256]{3,0,2,1:T(4,128)} fusion(f32[512,3,2,4,2,256]{5,0,4,3,2,1:T(8,128)} %fusion.8, f32[4,2,4,2,1,1,1]{0,2,1,6,5,4,3:T(4,128)S(1)} %fusion.116), kind=kOutput, calls=%fused_computation.3 | convolution fusion | flops 614989824 | bytes 31457536 | tf_op jit(solution)/shard_map/ctpyom,yoeq->ctpeqm/dot_general | solution.py:53
  220.2 7.6 %copy.32 = f32[512,3,4,256]{0,3,2,1:T(8,128)} copy(f32[512,3,4,256]{3,2,1,0:T(4,128)} %bitcast.87) | data formatting | bytes 12582912 | tf_op jit(solution)/shard_map/reduce_sum | solution.py:56
  227.7 10.3 %copy.33 = f32[512,3,1024]{0,1,2:T(4,128)} copy(f32[512,3,1024]{0,2,1:T(8,128)} %bitcast.86) | data formatting | bytes 12582912 | tf_op jit(solution)/shard_map/reshape | solution.py:57
  238.1 16.7 %gather_fusion.1 = f32[1024,512,3]{1,2,0:T(4,128)} fusion(f32[512,3,1024]{0,1,2:T(4,128)} %copy.33, s32[1024]{0:T(1024)S(1)} %fusion.68), kind=kCustom, calls=%fused_computation.1 | custom fusion | bytes 12587008 | tf_op jit(solution)/shard_map/jit(_take)/gather | solution.py:89
  254.8 9.1 %copy.34 = f32[1024,512,3]{0,1,2:T(8,128)} copy(f32[1024,512,3]{1,2,0:T(4,128)} %gather_fusion.1) | data formatting | bytes 12582912 | tf_op jit(solution)/shard_map/jit(_take)/gather | solution.py:89
  263.9 5.2 bitcast_reduce_fusion
  269.2 67.4 %all-reduce.4.cloned.1.call-done = f32[512,1024]{1,0:T(8,128)} async-done(((f32[512,1024]{1,0:T(8,128)}), f32[512,1024]{1,0:T(8,128)}) %all-reduce.4.cloned.1.call-update) | async-done | bytes 2097168 | tf_op jit(solution)/shard_map/psum | solution.py:90
  336.6 1.8 broadcast_multiply_fusion
  338.4 5.7 fusion.11
  344.2 1.5 collective-permute-start.1
  345.6 3.6 collective-permute-start
  350.1 6.6 %fusion.37 = f32[512,3,1024]{2,0,1:T(8,128)} fusion(bf16[512,3,1024]{2,0,1:T(8,128)(2,1)} %fusion.11, s32[512]{0:T(512)S(1)} %copy-done, s32[512]{0:T(512)S(1)} %dynamic_slice.3), kind=kOutput, calls=%fused_computation.44 | convolution fusion | flops 1613234176 | bytes 9441280 | tf_op jit(solution)/shard_map/ctb,cd->btd/dot_general | solution.py:73
  356.6 54.2 %collective-permute-done.1 = bf16[512,3,1024]{2,0,1:T(8,128)(2,1)S(1)} collective-permute-done((bf16[512,3,1024]{2,0,1:T(8,128)(2,1)}, bf16[512,3,1024]{2,0,1:T(8,128)(2,1)S(1)}, u32[]{:S(2)}, u32[]{:S(2)}) %collective-permute-start.1) | collective-permute-done | bytes 3145760 | tf_op jit(solution)/shard_map/ppermute | solution.py:22
  411.1 36.2 %collective-permute-done = bf16[512,3,1024]{2,0,1:T(8,128)(2,1)} collective-permute-done((bf16[512,3,1024]{2,0,1:T(8,128)(2,1)}, bf16[512,3,1024]{2,0,1:T(8,128)(2,1)}, u32[]{:S(2)}, u32[]{:S(2)}) %collective-permute-start) | collective-permute-done | bytes 3145760 | tf_op jit(solution)/shard_map/ppermute | solution.py:22
  447.4 2.2 constant_dynamic-update-slice_fusion
  449.6 4.5 fusion.20
  454.0 4.6 fusion.18
  458.6 7.1 %fusion.16 = f32[512,3,1024]{2,0,1:T(8,128)} fusion(bf16[512,3,1024]{2,0,1:T(8,128)(2,1)} %collective-permute-done, bf16[512,3,1024]{2,0,1:T(8,128)(2,1)} %fusion.11, s32[512]{0:T(512)S(1)} %copy-done, s32[512]{0:T(512)S(1)} %dynamic_slice.3), kind=kOutput, calls=%fused_computation.20 | convolution fusion | flops 1619525632 | bytes 12587008 | tf_op jit(solution)/shard_map/ctb,cd->btd/dot_general | solution.py:73
  465.7 7.1 %fusion.22 = f32[512,3,1024]{2,0,1:T(8,128)} fusion(bf16[512,3,1024]{2,0,1:T(8,128)(2,1)} %fusion.11, bf16[512,3,1024]{2,0,1:T(8,128)(2,1)} %collective-permute-done, s32[512]{0:T(512)S(1)} %copy-done, s32[512]{0:T(512)S(1)} %dynamic_slice.3), kind=kOutput, calls=%fused_computation.26 | convolution fusion | flops 1619525632 | bytes 12587008 | tf_op jit(solution)/shard_map/ctb,cd->btd/dot_general | solution.py:73
  472.8 6.4 %fusion.33 = f32[512,3,1024]{2,0,1:T(8,128)} fusion(bf16[512,3,1024]{2,0,1:T(8,128)(2,1)} %collective-permute-done, s32[512]{0:T(512)S(1)} %copy-done, s32[512]{0:T(512)S(1)} %dynamic_slice.3), kind=kOutput, calls=%fused_computation.40 | convolution fusion | flops 1613234176 | bytes 9441280 | tf_op jit(solution)/shard_map/ctb,cd->btd/dot_general | solution.py:73
  479.1 16.9 %add_bitcast_fusion = f32[1024,3,512]{0,2,1:T(8,128)} fusion(f32[512,3,1024]{2,0,1:T(8,128)} %fusion.18, f32[512,3,1024]{2,0,1:T(8,128)} %fusion.20, f32[512,3,1024]{2,0,1:T(8,128)} %fusion.33, f32[512,3,1024]{2,0,1:T(8,128)} %fusion.22, f32[512,3,1024]{2,0,1:T(8,128)} %fusion.37, f32[512,3,1024]{2,0,1:T(8,128)} %fusion.16, ...), kind=kOutput, calls=%fused_computation.17 | convolution fusion | flops 1622671360 | bytes 47190016 | tf_op jit(solution)/shard_map/ctb,cd->btd/dot_general | solution.py:73
  496.1 68.1 %reduce-scatter.2.cloned.1.call-done = f32[256,3,512]{0,2,1:T(8,128)} async-done(((f32[1024,3,512]{0,2,1:T(8,128)}), f32[256,3,512]{0,2,1:T(8,128)}) %reduce-scatter.2.cloned.1.call-update) | async-done | bytes 1572880 | tf_op jit(solution)/shard_map/reduce_scatter | solution.py:27
  564.2 3.0 copy.35
  568.4 57.2 %all-reduce.6.cloned.1.call-done = f32[256,3,512]{2,1,0:T(4,128)} async-done(((f32[256,3,512]{2,1,0:T(4,128)}), f32[256,3,512]{2,1,0:T(4,128)}) %all-reduce.6.cloned.1.call-update) | async-done | bytes 1572880
  625.6 1.1 constant_dynamic-slice_fusion
  626.7 0.9 copy_multiply_fusion
  (25 shorter events, 4.9 us)
Async XLA Ops:
  6.5 330.1 %all-reduce.4.cloned.1.call-start = ((), (), s32[]{:S(2)}) async-start(), calls=%async_computation.1 | async-start | bytes 4194304 | tf_op jit(solution)/shard_map/psum | solution.py:90
  269.1 295.0 %reduce-scatter.2.cloned.1.call-start = ((), (), s32[]{:S(2)}) async-start(), calls=%async_computation.2 | async-start | bytes 7864320 | tf_op jit(solution)/shard_map/reduce_scatter | solution.py:27
  338.4 11.6 %copy-start = (s32[512]{0:T(512)S(1)}, s32[512]{0:T(512)}, u32[]{:S(2)}) copy-start(s32[512]{0:T(512)} %param.8) | copy-start | bytes 6148
  344.2 66.7 %collective-permute-start.1 = (bf16[512,3,1024]{2,0,1:T(8,128)(2,1)}, bf16[512,3,1024]{2,0,1:T(8,128)(2,1)S(1)}, u32[]{:S(2)}, u32[]{:S(2)}) collective-permute-start(bf16[512,3,1024]{2,0,1:T(8,128)(2,1)} %fusion.11), channel_id=1, source_target_pairs={{0,2},{1,3},{2,4},{3,5},{4,6},{5,7},{8,10},{9,11},{10,12},{11,13},... | collective-permute-start | bytes 9437192 | tf_op jit(solution)/shard_map/ppermute | solution.py:22
  345.6 101.7 %collective-permute-start = (bf16[512,3,1024]{2,0,1:T(8,128)(2,1)}, bf16[512,3,1024]{2,0,1:T(8,128)(2,1)}, u32[]{:S(2)}, u32[]{:S(2)}) collective-permute-start(bf16[512,3,1024]{2,0,1:T(8,128)(2,1)} %fusion.11), channel_id=1, source_target_pairs={{0,1},{1,2},{2,3},{3,4},{4,5},{5,6},{6,7},{8,9},{9,10},{10,11},{11... | collective-permute-start | bytes 9437192 | tf_op jit(solution)/shard_map/ppermute | solution.py:22
  496.0 71.2 %copy-start.1 = (u32[128]{0:T(128)S(1)}, u32[128]{0:T(128)}, u32[]{:S(2)}) copy-start(u32[128]{0:T(128)} %constant.116) | copy-start | bytes 1540
  496.0 129.6 %all-reduce.6.cloned.1.call-start = ((), (), s32[]{:S(2)}) async-start(), calls=%async_computation.3 | async-start | bytes 4194304
Sparse Core Ops, SparseCore 0:
  269.3 67.3 all-reduce.3
  496.1 67.9 reduce-scatter.1
  567.3 58.2 all-reduce.5
where the time goes:
time: 643 us; the launch traced here: 634 us
  waiting for transfers between devices  283 us (44%)
  matrix products  158 us (25%)
  local copies, waits for them, and re-layouts  156 us (24%)
  other arithmetic  18.6 us (3%)
  between operations  14.1 us (2%)
    ppermute x2, waiting for transfers between devices, shifted(): lax.ppermute(value, axis, [(source, source + steps) for source in range(i...  90.4 us
    dot_general x1, matrix products, compute_power(): jnp.einsum('ctpyom,yoeq->ctpeqm', north_beams, west_table(), precision=la...  88.4 us
    reduce_scatter x1, waiting for transfers between devices, summed_rows(): total = lax.psum_scatter(total, axis, scatter_dimension=0, tiled=True)  68.1 us
    psum x1, waiting for transfers between devices, per_device(): totals = lax.psum(jnp.sum(ordered, axis=1), 'tm')  67.4 us
    gather x2, local copies, waits for them, and re-layouts, per_device(): jnp.take(voltages, slot_feed, axis=3)  61 us
    unnamed x4, waiting for transfers between devices  57.2 us
    dot_general x7, matrix products, shift_sum(): jnp.einsum('ctb,cd->btd', window, onehot, preferred_element_type=jnp.floa...  53 us
    unnamed x8, local copies, waits for them, and re-layouts  44.8 us
  transfers between devices with their start and end apart: 5, of which 5 were waited for; matrix products, arithmetic and copies ran while one was open for 1% of the time, Pallas kernels for 0%

commit v1 on v0

v1 whole, which is shorter than its diff:
```python
import functools
import math

import jax
import jax.numpy as jnp
from jax import lax
from jax.experimental import pallas as pl
from jax.experimental.pallas import tpu as pltpu
from jax.sharding import PartitionSpec as P

NS = 256
CYL = 4
POL = 2
CHANNELS = 8192
NDM = 512
MAXD = 6
QUANT = 2796202
FEEDS = 2048
BEAMS = 1024
TIME = 24
CHUNKS = 2
AXES = ("sub", "tm")


def north_table():
    positions = jnp.arange(NS, dtype=jnp.int32)
    phase_index = positions[:, None] * positions[None, :] % NS
    angles = phase_index.astype(jnp.float32) * (2.0 * math.pi / NS)
    cosine = jnp.cos(angles) / math.sqrt(NS)
    sine_part = jnp.sin(angles) / math.sqrt(NS)
    real_row = jnp.stack([cosine, -sine_part], axis=1)
    imag_row = jnp.stack([sine_part, cosine], axis=1)
    table = jnp.stack([real_row, imag_row], axis=0).astype(jnp.bfloat16)
    return table.reshape(2 * NS, 2 * NS)


def form_kernel(volt_ref, feed_ref, table_ref, order_ref, out_ref, grid_ref):
    chans = volt_ref.shape[0]
    rows = volt_ref[:, 0].reshape(2 * chans, FEEDS)
    half = NS // 2

    def slots(at, phase):
        tiles = [grid_ref[at // half + i, pl.ds(phase, chans, stride=2), :] for i in range(2)]
        return jnp.concatenate(tiles, axis=1).astype(jnp.bfloat16)

    placed = jnp.dot(rows, feed_ref[...], preferred_element_type=jnp.float32)
    for tile in range(FEEDS // half):
        grid_ref[tile] = placed[:, tile * half : (tile + 1) * half]
    power = [None] * CYL
    for p in range(POL):
        re, im = [], []
        for y in range(CYL):
            at = (p * CYL + y) * NS
            pair = jnp.concatenate([slots(at, 0), slots(at, 1)], axis=1)
            north = jnp.dot(pair, table_ref[...], preferred_element_type=jnp.float32)
            re.append(north[:, :NS])
            im.append(north[:, NS:])
        a_re, a_im = re[0] + re[2], im[0] + im[2]
        b_re, b_im = re[0] - re[2], im[0] - im[2]
        c_re, c_im = re[1] + re[3], im[1] + im[3]
        d_re, d_im = re[1] - re[3], im[1] - im[3]
        west = [
            (a_re + c_re, a_im + c_im),
            (b_re + d_im, b_im - d_re),
            (a_re - c_re, a_im - c_im),
            (b_re - d_im, b_im + d_re),
        ]
        for e, (w_re, w_im) in enumerate(west):
            square = w_re * w_re + w_im * w_im
            power[e] = square if power[e] is None else power[e] + square
    intensity = 0.25 * jnp.concatenate(power, axis=1)
    high = intensity.astype(jnp.bfloat16)
    rest = intensity - high.astype(jnp.float32)
    mid = rest.astype(jnp.bfloat16)
    low = (rest - mid.astype(jnp.float32)).astype(jnp.bfloat16)
    total = None
    for piece in (high, mid, low):
        part = lax.dot_general(
            order_ref[...], piece, (((1,), (1,)), ((), ())), preferred_element_type=jnp.float32
        )
        total = part if total is None else total + part
    out_ref[...] = total.reshape(out_ref.shape)


def form_beams(voltages, feed_onehot, table, order_onehot, chunk, chans):
    samples = voltages.shape[1]
    block = 256
    steps = chans // block
    first = chunk * steps
    groups = BEAMS // 8
    whole = pl.BlockSpec(memory_space=pltpu.VMEM)
    return pl.pallas_call(
        form_kernel,
        grid=(steps, samples),
        in_specs=[
            pl.BlockSpec((block, 1, 2, FEEDS), lambda c, t: (first + c, t, 0, 0)),
            whole,
            whole,
            whole,
        ],
        out_specs=pl.BlockSpec((groups, 1, 8, block), lambda c, t: (0, t, 0, c)),
        out_shape=jax.ShapeDtypeStruct((groups, samples, 8, chans), jnp.float32),
        scratch_shapes=[pltpu.VMEM((FEEDS // 128, 2 * block, 128), jnp.float32)],
        compiler_params=pltpu.CompilerParams(vmem_limit_bytes=56 * 2**20),
        cost_estimate=pl.CostEstimate(
            flops=int(2 * chans * samples * (2 * FEEDS * FEEDS + 8 * 512 * 512 + 3 * BEAMS * BEAMS)),
            bytes_accessed=chans * samples * 2 * FEEDS * 4,
            transcendentals=0,
        ),
        name="form_beams",
    )(voltages, feed_onehot, table, order_onehot)


def sum_kernel(last, held_ref, lag_ref, trial_ref, before_ref, out_ref):
    chans = held_ref.shape[-1]
    step = pl.program_id(0)

    @pl.when(step == 0)
    def _():
        out_ref[...] = before_ref[...]

    held = held_ref[...].reshape(TIME, 8, chans)
    average = jnp.sum(held, axis=0) / TIME
    normal = (held - average[None]).reshape(TIME * 8, chans).astype(jnp.bfloat16)
    lag_rows = jnp.broadcast_to(lag_ref[0], (8, chans))
    lag = jnp.transpose(lag_rows)[:, :1]
    product = lag * trial_ref[...]
    delay = jnp.floor(product * (1.0 / QUANT)).astype(jnp.bfloat16)
    for k in range(MAXD + 1):
        onehot = jnp.where(delay == k, 1.0, 0.0).astype(jnp.bfloat16)
        keep = TIME * 8 - 8 * k
        rows = -(-keep // 16) * 16
        part = jnp.dot(normal[:rows], onehot, preferred_element_type=jnp.float32)
        out_ref[8 * k :, :] += part[:keep]

    if last:

        @pl.when(step == pl.num_programs(0) - 1)
        def _():
            out_ref[...] = out_ref[...] * (1.0 / math.sqrt(CHANNELS))


def sum_delays(held, lags, trials, before, last):
    chans = held.shape[-1]
    subs = lags.shape[0]
    shards = held.shape[0] // subs
    samples = held.shape[1]
    rows = TIME * 8
    return pl.pallas_call(
        functools.partial(sum_kernel, last),
        grid=(subs,),
        in_specs=[
            pl.BlockSpec((shards, samples, 8, chans), lambda s: (s, 0, 0, 0)),
            pl.BlockSpec((1, 1, chans), lambda s: (s, 0, 0)),
            pl.BlockSpec(memory_space=pltpu.VMEM),
            pl.BlockSpec(memory_space=pltpu.VMEM),
        ],
        out_specs=pl.BlockSpec((rows, NDM), lambda s: (0, 0)),
        out_shape=jax.ShapeDtypeStruct((rows, NDM), jnp.float32),
        compiler_params=pltpu.CompilerParams(vmem_limit_bytes=48 * 2**20),
        cost_estimate=pl.CostEstimate(
            flops=2 * subs * chans * rows * NDM * 7,
            bytes_accessed=subs * chans * rows * 4,
            transcendentals=0,
        ),
        name="sum_delays",
    )(held, lags, trials, before)


def per_device(voltages, slot_feed, chan_lag, trial_dm, beam_order):
    samples = voltages.shape[1]
    subs, shards = lax.axis_size("sub"), lax.axis_size("tm")
    feeds = jnp.arange(FEEDS, dtype=jnp.int32)
    feed_onehot = (feeds[:, None] == slot_feed[None, :]).astype(jnp.bfloat16)
    beams = jnp.arange(BEAMS, dtype=jnp.int32)
    order_onehot = (beam_order[:, None] == beams[None, :]).astype(jnp.bfloat16)
    table = north_table()
    lags = chan_lag.astype(jnp.float32).reshape(subs, CHUNKS, -1)
    trials = trial_dm.astype(jnp.float32).reshape(1, NDM)
    chans = voltages.shape[0] // CHUNKS
    total = jnp.zeros((TIME * 8, NDM), jnp.float32)
    for chunk in range(CHUNKS):
        formed = form_beams(voltages, feed_onehot, table, order_onehot, chunk, chans)
        held = lax.all_to_all(formed, AXES, 0, 0)
        total = sum_delays(held, lags[:, chunk : chunk + 1], trials, total, chunk == CHUNKS - 1)
    parts = lax.all_to_all(total.reshape(shards, samples, 8, NDM), "tm", 0, 0)
    return parts.transpose(0, 2, 1, 3).reshape(shards * 8, samples, NDM)


def solution(mesh):
    placed = (P("sub", "tm", None, None), P(), P(), P(), P())
    return jax.shard_map(
        per_device, mesh=mesh, in_specs=placed, out_specs=P("sub", "tm", None), check_vma=False
    )
```

time: 643 us -> 176 us (0.27); the launches traced: 634 us -> 175 us
  waiting for transfers between devices: 283 us -> 33.9 us
  matrix products: 158 us -> 0 us
  local copies, waits for them, and re-layouts: 156 us -> 4.05 us
  Pallas kernels: 0 us -> 96.9 us
  between operations: 14.1 us -> 0.14 us
  starting transfers between devices: 5.2 us -> 17.3 us
  blocking collectives: 0 us -> 11.8 us
  other arithmetic: 18.6 us -> 11.3 us
    dot_general x9 -> x0, matrix products: 158 us -> none  [the longest x1 88.4 us: compute_power(): jnp.einsum('ctpyom,yoeq->ctpeqm', north_beams, west_table(), precision=la...]
    pallas_call x0 -> x4, Pallas kernels: none -> 96.9 us  [the longest x2 58 us: form_beams(): pl.pallas_call(form_kernel, grid=(steps, samples), in_specs=[pl.BlockSpec...]
    ppermute x2 -> x0, waiting for transfers between devices: 90.4 us -> none  [shifted(): lax.ppermute(value, axis, [(source, source + steps) for source in range(i...]
    gather x4 -> x0, local copies, waits for them, and re-layouts: 86.8 us -> none  [the longest x2 61 us: per_device(): jnp.take(voltages, slot_feed, axis=3)]
    reduce_scatter x1 -> x0, waiting for transfers between devices: 68.1 us -> none  [summed_rows(): total = lax.psum_scatter(total, axis, scatter_dimension=0, tiled=True)]
    psum x1 -> x0, waiting for transfers between devices: 67.4 us -> none  [per_device(): totals = lax.psum(jnp.sum(ordered, axis=1), 'tm')]
    unnamed x4 -> x0, waiting for transfers between devices: 57.2 us -> none
    unnamed x8 -> x13, local copies, waits for them, and re-layouts: 44.8 us -> 2.65 us
  transfers between devices with their start and end apart: 5 -> 2, of which waited for: 5 -> 2; matrix products, arithmetic and copies ran while one was open for 1% -> 0% of each run, Pallas kernels for 0% -> 27%
where the time goes in v1:
time: 176 us; the launch traced here: 175 us
  Pallas kernels  96.9 us (55%)
  waiting for transfers between devices  33.9 us (19%)
  starting transfers between devices  17.3 us (10%)
  blocking collectives  11.8 us (7%)
  other arithmetic  11.3 us (6%)
  local copies, waits for them, and re-layouts  4.05 us (2%)
    pallas_call x2, Pallas kernels, form_beams(): pl.pallas_call(form_kernel, grid=(steps, samples), in_specs=[pl.BlockSpec...  58 us
    pallas_call x2, Pallas kernels, sum_delays(): pl.pallas_call(functools.partial(sum_kernel, last), grid=(subs,), in_spec...  38.9 us
    all_to_all x2, waiting for transfers between devices, per_device(): held = lax.all_to_all(formed, AXES, 0, 0)  33.9 us
    all_to_all x2, starting transfers between devices, per_device(): held = lax.all_to_all(formed, AXES, 0, 0)  17.3 us
    all_to_all x1, blocking collectives, per_device(): parts = lax.all_to_all(total.reshape(shards, samples, 8, NDM), 'tm', 0, 0)  11.8 us
    convert_element_type x1, other arithmetic, per_device(): feed_onehot = (feeds[:, None] == slot_feed[None, :]).astype(jnp.bfloat16)  7.39 us
  transfers between devices with their start and end apart: 2, of which 2 were waited for; matrix products, arithmetic and copies ran while one was open for 0% of the time, Pallas kernels for 27%

profile of v1, /device:TPU:1, one launch (start us, length us, event | category | flops | bytes accessed | tf_op | source)
XLA Modules:
  0.0 175.2 jit_solution(14489379136562729022)
XLA Ops:
  0.0 0.0 copy-start.3
  0.0 1.1 negate_convert_fusion
  1.1 1.0 fusion.8
  2.2 0.1 pad_maximum_fusion
  2.2 0.5 copy.7
  2.8 0.9 copy.9
  3.7 0.0 copy-done.3
  3.7 0.0 copy-start.4
  3.7 7.4 %fusion.feed_ref = bf16[2048,2048]{1,0:T(8,128)(2,1)} fusion(s32[2048]{0:T(1024)S(1)} %copy-done.3), kind=kLoop, calls=%fused_computation.1 | loop fusion | flops 8388608 | bytes 8396800 | tf_op jit(solution)/shard_map/convert_element_type | solution.py:174
  11.1 0.0 copy-done.4
  11.1 1.7 fusion.1.order_ref
  12.8 29.0 %form_beams.3 = f32[128,3,8,256]{3,2,1,0:T(8,128)} custom-call(bf16[512,3,2,2048]{3,2,1,0:T(2,128)(2,1)} %volt_ref.3, bf16[2048,2048]{1,0:T(8,128)(2,1)} %fusion.feed_ref, bf16[512,512]{1,0:T(8,128)(2,1)} %bitcast.18, bf16[1024,1024]{1,0:T(8,128)(2,1)} %fusion.1.order_ref), custom_call_target="tpu_custom_call" | custom-call | flops 20937965568 | bytes 12582912 | tf_op jit(solution)/shard_map/form_beams/pallas_call | solution.py:92
  41.7 11.5 %all-to-all-start.1 = ((f32[128,3,8,256]{3,2,1,0:T(8,128)}), f32[128,3,8,256]{3,2,1,0:T(8,128)S(1)}, u32[]{:S(2)}, u32[]{:S(2)}) async-start(f32[128,3,8,256]{3,2,1,0:T(8,128)} %form_beams.3), calls=%async_computation.1 | async-start | bytes 6291456 | tf_op jit(solution)/shard_map/all_to_all | solution.py:184
  53.2 29.0 %form_beams.2 = f32[128,3,8,256]{3,2,1,0:T(8,128)} custom-call(bf16[512,3,2,2048]{3,2,1,0:T(2,128)(2,1)} %volt_ref.3, bf16[2048,2048]{1,0:T(8,128)(2,1)} %fusion.feed_ref, bf16[512,512]{1,0:T(8,128)(2,1)} %bitcast.19, bf16[1024,1024]{1,0:T(8,128)(2,1)} %fusion.1.order_ref), custom_call_target="tpu_custom_call" | custom-call | flops 20937965568 | bytes 12582912 | tf_op jit(solution)/shard_map/form_beams/pallas_call | solution.py:92
  82.2 0.0 copy-start.2
  82.2 0.0 copy-start.5
  82.2 12.4 %all-to-all-done.1.held_ref = f32[128,3,8,256]{3,2,1,0:T(8,128)S(1)} async-done(((f32[128,3,8,256]{3,2,1,0:T(8,128)}), f32[128,3,8,256]{3,2,1,0:T(8,128)S(1)}, u32[]{:S(2)}, u32[]{:S(2)}) %all-to-all-start.1) | async-done | bytes 3145760 | tf_op jit(solution)/shard_map/all_to_all | solution.py:184
  94.7 5.8 %all-to-all-start = ((f32[128,3,8,256]{3,2,1,0:T(8,128)}), f32[128,3,8,256]{3,2,1,0:T(8,128)}, u32[]{:S(2)}, u32[]{:S(2)}) async-start(f32[128,3,8,256]{3,2,1,0:T(8,128)} %form_beams.2), calls=%async_computation | async-start | bytes 6291456 | tf_op jit(solution)/shard_map/all_to_all | solution.py:184
  100.4 0.0 copy-done.2
  100.5 0.0 copy-done.5
  100.6 18.9 %sum_delays.2.before_ref = f32[192,512]{1,0:T(8,128)S(1)} custom-call(f32[128,3,8,256]{3,2,1,0:T(8,128)S(1)} %all-to-all-done.1.held_ref, f32[16,1,256]{2,1,0:T(1,128)S(1)} %get-tuple-element.7.lag_ref, f32[1,512]{1,0:T(1,128)S(1)} %bitcast.15, f32[192,512]{1,0:T(8,128)S(1)} %broadcast_in_dim.2.before_ref), custom_call_target="tpu_custom_call" | custom-call | flops 5637144576 | bytes 3145728 | tf_op jit(solution)/shard_map/sum_delays/pallas_call | solution.py:149
  119.5 0.0 copy-start
  119.5 0.7 copy-done
  120.3 21.4 %all-to-all-done.held_ref = f32[128,3,8,256]{3,2,1,0:T(8,128)} async-done(((f32[128,3,8,256]{3,2,1,0:T(8,128)}), f32[128,3,8,256]{3,2,1,0:T(8,128)}, u32[]{:S(2)}, u32[]{:S(2)}) %all-to-all-start) | async-done | bytes 3145760 | tf_op jit(solution)/shard_map/all_to_all | solution.py:184
  141.7 0.0 copy-start.1
  141.7 1.0 copy-done.1
  142.7 20.0 %sum_delays.3 = f32[192,512]{1,0:T(8,128)S(1)} custom-call(f32[128,3,8,256]{3,2,1,0:T(8,128)} %all-to-all-done.held_ref, f32[16,1,256]{2,1,0:T(1,128)S(1)} %get-tuple-element.8.lag_ref, f32[1,512]{1,0:T(1,128)S(1)} %bitcast.16, f32[192,512]{1,0:T(8,128)S(1)} %copy-done.1), custom_call_target="tpu_custom_call" | custom-call | flops 5637144576 | bytes 3145728 | tf_op jit(solution)/shard_map/sum_delays/pallas_call | solution.py:149
  162.7 11.8 %all_to_all.15 = f32[8,3,8,512]{3,2,1,0:T(8,128)S(1)} all-to-all(f32[8,3,8,512]{3,2,1,0:T(8,128)S(1)} %bitcast.14), channel_id=1, replica_groups=mesh['sub'=16,'tm'=8] {'tm'}, dimensions={0} | all-to-all | bytes 786432 | tf_op jit(solution)/shard_map/all_to_all | solution.py:186
  174.5 0.8 copy_bitcast_fusion
  (6 shorter events, 0.1 us)
Async XLA Ops:
  0.0 3.7 %copy-start.3 = (s32[2048]{0:T(1024)S(1)}, s32[2048]{0:T(1024)}, u32[]{:S(2)}) copy-start(s32[2048]{0:T(1024)} %param.6) | copy-start | bytes 24580
  3.7 7.4 %copy-start.4 = (s32[1024]{0:T(1024)S(1)}, s32[1024]{0:T(1024)}, u32[]{:S(2)}) copy-start(s32[1024]{0:T(1024)} %param.9) | copy-start | bytes 12292
  41.7 52.9 %all-to-all-start.1 = ((f32[128,3,8,256]{3,2,1,0:T(8,128)}), f32[128,3,8,256]{3,2,1,0:T(8,128)S(1)}, u32[]{:S(2)}, u32[]{:S(2)}) async-start(f32[128,3,8,256]{3,2,1,0:T(8,128)} %form_beams.3), calls=%async_computation.1 | async-start | bytes 6291456 | tf_op jit(solution)/shard_map/all_to_all | solution.py:184
  82.2 18.2 %copy-start.2 = (s32[8192]{0:T(1024)S(1)}, s32[8192]{0:T(1024)}, u32[]{:S(2)}) copy-start(s32[8192]{0:T(1024)} %param.7) | copy-start | bytes 98308
  82.2 18.3 %copy-start.5 = (s32[512]{0:T(512)S(1)}, s32[512]{0:T(512)}, u32[]{:S(2)}) copy-start(s32[512]{0:T(512)} %param.8) | copy-start | bytes 6148
  94.7 47.0 %all-to-all-start = ((f32[128,3,8,256]{3,2,1,0:T(8,128)}), f32[128,3,8,256]{3,2,1,0:T(8,128)}, u32[]{:S(2)}, u32[]{:S(2)}) async-start(f32[128,3,8,256]{3,2,1,0:T(8,128)} %form_beams.2), calls=%async_computation | async-start | bytes 6291456 | tf_op jit(solution)/shard_map/all_to_all | solution.py:184
  119.5 0.7 copy-start
  141.7 1.0 copy-start.1

commit v2 on v1

v2 whole, which is shorter than its diff:
```python
import functools
import math

import jax
import jax.numpy as jnp
import ml_dtypes
import numpy as np
from jax import lax
from jax.experimental import pallas as pl
from jax.experimental.pallas import tpu as pltpu
from jax.sharding import PartitionSpec as P

NS = 256
CYL = 4
POL = 2
CHANNELS = 8192
NDM = 512
MAXD = 6
QUANT = 2796202
FEEDS = 2048
BEAMS = 1024
TIME = 24
CHUNKS = 2
LEVELS = 65535.0
HALF = 32768.0
STEPS = 256.0
GROUPS = 8
ROOM = 64
SAMPLE_ROWS = 48
ROWS = 56
AXES = ("sub", "tm")


def half_table():
    n = np.arange(NS)[:, None]
    m = np.arange(NS // 2)[None, :]
    angles = (n * m % NS) * (2.0 * math.pi / NS)
    cosine = np.cos(angles) / math.sqrt(NS)
    sine = np.sin(angles) / math.sqrt(NS)
    sine[:, 0] = np.cos((np.arange(NS) * (NS // 2) % NS) * (2.0 * math.pi / NS)) / math.sqrt(NS)
    return np.concatenate([cosine, sine], axis=1).astype(np.float32).astype(ml_dtypes.bfloat16)


def as_onehot(hit):
    return hit.astype(jnp.float32).astype(jnp.bfloat16)


def column_of(row):
    return jnp.transpose(jnp.broadcast_to(row, (8, row.shape[1])))[:, :1]


def route_kernel(feed_ref, order_ref, table_ref, first_ref, second_ref, pick_ref, deepest_ref):
    deepest = jnp.zeros((), jnp.int32)
    codes = []
    above = lax.broadcasted_iota(jnp.int32, (NS, NS), 0) < lax.broadcasted_iota(jnp.int32, (NS, NS), 1)
    for d in range(GROUPS):
        block = feed_ref[:, d * NS : (d + 1) * NS] // NS
        same = (column_of(block) == block) & above
        rank = jnp.sum(same.astype(jnp.float32), axis=0, keepdims=True).astype(jnp.int32)
        deepest = jnp.maximum(deepest, jnp.max(rank))
        odd = block % 2
        flip = odd if d % 2 == 0 else 1 - odd
        codes.append((jnp.where(odd == 0, d, d ^ 1)) * ROOM + rank)
        place = block // 2 * (2 * ROOM) + flip * ROOM + rank
        hit = lax.broadcasted_iota(jnp.int32, (GROUPS * ROOM, NS), 0) == place
        second_ref[d] = jnp.dot(
            as_onehot(hit), table_ref[...], preferred_element_type=jnp.float32
        ).astype(jnp.bfloat16)
    code = jnp.concatenate(codes, axis=1).astype(jnp.float32)
    for b in range(GROUPS):
        feeds = lax.broadcasted_iota(jnp.int32, (NS, FEEDS), 0) + b * NS
        mine = jnp.sum(jnp.where(feeds == feed_ref[...], code, 0.0), axis=1, keepdims=True)
        lanes = lax.broadcasted_iota(jnp.int32, (NS, GROUPS * ROOM), 1)
        first_ref[b] = as_onehot(mine.astype(jnp.int32) == lanes)
    north = order_ref[...] % NS
    wanted = order_ref[...] - north + jnp.where(north <= NS // 2, north, NS + NS // 2 - north)
    pick_ref[...] = as_onehot(column_of(wanted) == lax.broadcasted_iota(jnp.int32, (BEAMS, BEAMS), 1))
    deepest_ref[0] = deepest


def route(slot_feed, beam_order, table):
    whole = pl.BlockSpec(memory_space=pltpu.VMEM)
    return pl.pallas_call(
        route_kernel,
        in_specs=[whole, whole, whole],
        out_specs=[whole, whole, whole, pl.BlockSpec(memory_space=pltpu.SMEM)],
        out_shape=[
            jax.ShapeDtypeStruct((GROUPS, NS, GROUPS * ROOM), jnp.bfloat16),
            jax.ShapeDtypeStruct((GROUPS, GROUPS * ROOM, NS), jnp.bfloat16),
            jax.ShapeDtypeStruct((BEAMS, BEAMS), jnp.bfloat16),
            jax.ShapeDtypeStruct((1,), jnp.int32),
        ],
        compiler_params=pltpu.CompilerParams(vmem_limit_bytes=56 * 2**20),
        name="route",
    )(slot_feed, beam_order, table)


def form_kernel(
    volt_ref, feed_ref, table_ref, first_ref, second_ref, pick_ref, deepest_ref, out_ref, grid_ref, unit_ref
):
    chans = volt_ref.shape[0]
    half = NS // 2
    t = pl.program_id(1)

    @pl.when(t == 0)
    def _():
        unit_ref[...] = jnp.zeros_like(unit_ref)

    @pl.when(deepest_ref[0] < ROOM)
    def _():
        rows = volt_ref[:, 0].reshape(2 * chans, FEEDS)
        low_half = lax.broadcasted_iota(jnp.int32, (2 * chans, half), 1) < ROOM
        pieces = [[] for _ in range(GROUPS)]
        for q in range(GROUPS // 2):
            ways = []
            for b in (2 * q, 2 * q + 1):
                way = jnp.dot(
                    rows[:, b * NS : (b + 1) * NS], first_ref[b], preferred_element_type=jnp.float32
                )
                ways.append(way)
            for v in range(GROUPS // 2):
                one = ways[0][:, v * half : (v + 1) * half]
                two = ways[1][:, v * half : (v + 1) * half]
                pieces[2 * v].append(jnp.where(low_half, one, two).astype(jnp.bfloat16))
                pieces[2 * v + 1].append(jnp.where(low_half, two, one).astype(jnp.bfloat16))
        for d in range(GROUPS):
            wave = jnp.dot(
                jnp.concatenate(pieces[d], axis=1), second_ref[d], preferred_element_type=jnp.float32
            )
            grid_ref[2 * d] = wave[:, :half]
            grid_ref[2 * d + 1] = wave[:, half:]

    @pl.when(deepest_ref[0] >= ROOM)
    def _():
        rows = volt_ref[:, 0].reshape(2 * chans, FEEDS)
        for d in range(GROUPS):
            feeds = lax.broadcasted_iota(jnp.int32, (FEEDS, NS), 0)
            place = as_onehot(feeds == feed_ref[:, d * NS : (d + 1) * NS])
            slots = jnp.dot(rows, place, preferred_element_type=jnp.float32).astype(jnp.bfloat16)
            wave = jnp.dot(slots, table_ref[...], preferred_element_type=jnp.float32)
            grid_ref[2 * d] = wave[:, :half]
            grid_ref[2 * d + 1] = wave[:, half:]

    edge = lax.broadcasted_iota(jnp.int32, (chans, half), 1) == 0

    def west(p, part):
        re, im = [], []
        for y in range(CYL):
            tile = 2 * (p * CYL + y) + part
            re.append(grid_ref[tile, pl.ds(0, chans, stride=2), :])
            im.append(grid_ref[tile, pl.ds(1, chans, stride=2), :])
        a_re, a_im = re[0] + re[2], im[0] + im[2]
        b_re, b_im = re[0] - re[2], im[0] - im[2]
        c_re, c_im = re[1] + re[3], im[1] + im[3]
        d_re, d_im = re[1] - re[3], im[1] - im[3]
        return [
            (a_re + c_re, a_im + c_im),
            (b_re + d_im, b_im - d_re),
            (a_re - c_re, a_im - c_im),
            (b_re - d_im, b_im + d_re),
        ]

    power = [None] * (2 * CYL)
    for p in range(POL):
        for e, ((c_re, c_im), (s_re, s_im)) in enumerate(zip(west(p, 0), west(p, 1))):
            t_re, t_im = jnp.where(edge, 0.0, s_re), jnp.where(edge, 0.0, s_im)
            u_re, u_im = c_re + t_im, c_im - t_re
            v_re, v_im = jnp.where(edge, s_re, c_re - t_im), jnp.where(edge, s_im, c_im + t_re)
            for at, (w_re, w_im) in ((2 * e, (u_re, u_im)), (2 * e + 1, (v_re, v_im))):
                square = w_re * w_re + w_im * w_im
                power[at] = square if power[at] is None else power[at] + square
    power = jnp.concatenate(power, axis=1)
    most = jnp.maximum(jnp.max(power, axis=1, keepdims=True), 1e-30)
    level = jnp.ceil(jnp.log2(most) * STEPS) + 1.0
    scale = LEVELS * jnp.exp2(level * (-1.0 / STEPS))
    code = jnp.floor(power * scale + 0.5)
    high = jnp.floor(code * (1.0 / 256.0)) * 256.0
    low = (code - high).astype(jnp.bfloat16)
    total = None
    for piece in (high.astype(jnp.bfloat16), low):
        part = lax.dot_general(
            pick_ref[...], piece, (((1,), (1,)), ((), ())), preferred_element_type=jnp.float32
        )
        total = part if total is None else total + part
    total = (total - HALF).reshape(BEAMS // 8, 8, chans)
    both = jnp.concatenate([total[:, :, : chans // 2], total[:, :, chans // 2 :]], axis=1)
    out_ref[:, pl.ds(pl.multiple_of(16 * t, 16), 16), :] = both.astype(jnp.int32).astype(jnp.int16)
    levels = jnp.transpose(jnp.broadcast_to(level, (chans, 128)))[:1]
    unit_ref[pl.ds(2 * t, 1), :] = levels[:, : chans // 2]
    unit_ref[pl.ds(2 * t + 1, 1), :] = levels[:, chans // 2 :]

    @pl.when(t == pl.num_programs(1) - 1)
    def _():
        levels = jnp.concatenate([unit_ref[...], jnp.zeros_like(unit_ref)], axis=0)
        levels = levels.astype(jnp.int32).astype(jnp.int16)
        groups = out_ref.shape[0]
        out_ref[:, SAMPLE_ROWS:, :] = jnp.broadcast_to(
            levels[None, : out_ref.shape[1] - SAMPLE_ROWS], (groups, out_ref.shape[1] - SAMPLE_ROWS, chans // 2)
        )


def form_beams(voltages, slot_feed, table, first, second, pick, deepest, chunk, chans):
    samples = voltages.shape[1]
    block = 256
    steps = chans // block
    base = chunk * steps
    groups = BEAMS // 8
    whole = pl.BlockSpec(memory_space=pltpu.VMEM)
    return pl.pallas_call(
        form_kernel,
        grid=(steps, samples),
        in_specs=[
            pl.BlockSpec((block, 1, 2, FEEDS), lambda c, t: (base + c, t, 0, 0)),
            whole,
            whole,
            whole,
            whole,
            whole,
            pl.BlockSpec(memory_space=pltpu.SMEM),
        ],
        out_specs=pl.BlockSpec((groups, ROWS, block // 2), lambda c, t: (0, 0, c)),
        out_shape=jax.ShapeDtypeStruct((groups, ROWS, chans // 2), jnp.int16),
        scratch_shapes=[
            pltpu.VMEM((FEEDS // 128, 2 * block, 128), jnp.float32),
            pltpu.VMEM((8, block // 2), jnp.float32),
        ],
        compiler_params=pltpu.CompilerParams(vmem_limit_bytes=56 * 2**20),
        cost_estimate=pl.CostEstimate(
            flops=int(2 * chans * samples * (2 * FEEDS * 512 + 2 * 8 * 512 * 256 + 2 * BEAMS * BEAMS)),
            bytes_accessed=chans * samples * 2 * FEEDS * 4,
            transcendentals=0,
        ),
        name="form_beams",
    )(voltages, slot_feed, table, first, second, pick, deepest)


def sum_kernel(last, held_ref, lag_ref, trial_ref, before_ref, out_ref):
    chans = 2 * held_ref.shape[-1]
    step = pl.program_id(0)

    @pl.when(step == 0)
    def _():
        out_ref[...] = before_ref[...]

    shards = held_ref.shape[0]
    code = held_ref[:, :SAMPLE_ROWS, :].reshape(TIME, 16, chans // 2).astype(jnp.float32) + HALF
    code = jnp.concatenate([code[:, :8], code[:, 8:]], axis=2)
    level = held_ref[:, SAMPLE_ROWS:, :].astype(jnp.float32)
    unit = jnp.exp2(level[:, :8] * (1.0 / STEPS)) * (0.25 / LEVELS)
    parts = []
    for shard in range(shards):
        for t in range(TIME // shards):
            row = jnp.concatenate(
                [unit[shard, 2 * t : 2 * t + 1], unit[shard, 2 * t + 1 : 2 * t + 2]], axis=1
            )
            parts.append(code[shard * (TIME // shards) + t] * row)
    held = jnp.stack(parts)
    average = jnp.sum(held, axis=0) / TIME
    normal = (held - average[None]).reshape(TIME * 8, chans).astype(jnp.bfloat16)
    lag = jnp.transpose(jnp.broadcast_to(lag_ref[0], (8, chans)))[:, :1]
    product = lag * trial_ref[...]
    delay = jnp.floor(product * (1.0 / QUANT)).astype(jnp.bfloat16)
    one, zero = jnp.ones((), jnp.bfloat16), jnp.zeros((), jnp.bfloat16)
    for k in range(MAXD + 1):
        onehot = jnp.where(delay == jnp.bfloat16(k), one, zero)
        keep = TIME * 8 - 8 * k
        rows = -(-keep // 16) * 16
        part = jnp.dot(normal[:rows], onehot, preferred_element_type=jnp.float32)
        out_ref[8 * k :, :] += part[:keep]

    if last:

        @pl.when(step == pl.num_programs(0) - 1)
        def _():
            out_ref[...] = out_ref[...] * (1.0 / math.sqrt(CHANNELS))


def sum_delays(held, lags, trials, before, last):
    chans = 2 * held.shape[-1]
    subs = lags.shape[0]
    shards = held.shape[0] // subs
    rows = TIME * 8
    return pl.pallas_call(
        functools.partial(sum_kernel, last),
        grid=(subs,),
        in_specs=[
            pl.BlockSpec((shards, ROWS, chans // 2), lambda s: (s, 0, 0)),
            pl.BlockSpec((1, 1, chans), lambda s: (s, 0, 0)),
            pl.BlockSpec(memory_space=pltpu.VMEM),
            pl.BlockSpec(memory_space=pltpu.VMEM),
        ],
        out_specs=pl.BlockSpec((rows, NDM), lambda s: (0, 0)),
        out_shape=jax.ShapeDtypeStruct((rows, NDM), jnp.float32),
        compiler_params=pltpu.CompilerParams(vmem_limit_bytes=56 * 2**20),
        cost_estimate=pl.CostEstimate(
            flops=2 * subs * chans * rows * NDM * 7,
            bytes_accessed=subs * chans * rows * 2,
            transcendentals=0,
        ),
        name="sum_delays",
    )(held, lags, trials, before)


def per_device(voltages, slot_feed, chan_lag, trial_dm, beam_order):
    samples = voltages.shape[1]
    subs, shards = lax.axis_size("sub"), lax.axis_size("tm")
    table = jnp.asarray(half_table())
    lags = chan_lag.astype(jnp.float32).reshape(subs, CHUNKS, -1)
    trials = trial_dm.astype(jnp.float32).reshape(1, NDM)
    feeds = slot_feed.reshape(1, FEEDS)
    order = beam_order.reshape(1, BEAMS)
    chans = voltages.shape[0] // CHUNKS
    total = jnp.zeros((TIME * 8, NDM), jnp.float32)
    first, second, pick, deepest = route(feeds, order, table)
    for chunk in range(CHUNKS):
        formed = form_beams(voltages, feeds, table, first, second, pick, deepest, chunk, chans)
        held = lax.all_to_all(formed, AXES, 0, 0)
        total = sum_delays(held, lags[:, chunk : chunk + 1], trials, total, chunk == CHUNKS - 1)
    parts = lax.all_to_all(total.reshape(shards, samples, 8, NDM), "tm", 0, 0)
    return parts.transpose(0, 2, 1, 3).reshape(shards * 8, samples, NDM)


def solution(mesh):
    placed = (P("sub", "tm", None, None), P(), P(), P(), P())
    return jax.shard_map(
        per_device, mesh=mesh, in_specs=placed, out_specs=P("sub", "tm", None), check_vma=False
    )
```

time: 176 us -> 128 us (0.73)
  Pallas kernels: 96.9 us -> 76.4 us
  waiting for transfers between devices: 33.9 us -> 17.8 us
  other arithmetic: 11.3 us -> 0.6 us
  local copies, waits for them, and re-layouts: 4.05 us -> 2.25 us
    pallas_call x2, Pallas kernels: 58 us -> 39.1 us  [form_beams(): pl.pallas_call(form_kernel, grid=(steps, samples), in_specs=[pl.BlockSpec...]
    all_to_all x2, waiting for transfers between devices: 33.9 us -> 17.8 us  [per_device(): held = lax.all_to_all(formed, AXES, 0, 0)]
    convert_element_type x2 -> x0, other arithmetic: 9.09 us -> none  [the longest x1 7.39 us: per_device(): feed_onehot = (feeds[:, None] == slot_feed[None, :]).astype(jnp.bfloat16)]
    pallas_call x2, Pallas kernels: 38.9 us -> 30.9 us  [sum_delays(): pl.pallas_call(functools.partial(sum_kernel, last), grid=(subs,), in_spec...]
    pallas_call x0 -> x1, Pallas kernels: none -> 6.47 us  [route(): pl.pallas_call(route_kernel, in_specs=[whole, whole, whole], out_specs=[w...]
    unnamed x13 -> x6, local copies, waits for them, and re-layouts: 2.65 us -> 0.01 us
    another operation x4 -> x0, other arithmetic: 2.19 us -> none
  transfers between devices with their start and end apart: 2 -> 2, of which waited for: 2 -> 2; matrix products, arithmetic and copies ran while one was open for 0% -> 2% of each run, Pallas kernels for 27% -> 27%
where the time goes in v2:
time: 128 us; the launch traced here: 127 us
  Pallas kernels  76.4 us (60%)
  waiting for transfers between devices  17.8 us (14%)
  starting transfers between devices  17.2 us (13%)
  blocking collectives  12.7 us (10%)
  local copies, waits for them, and re-layouts  2.25 us (2%)
    pallas_call x2, Pallas kernels, form_beams(): pl.pallas_call(form_kernel, grid=(steps, samples), in_specs=[pl.BlockSpec...  39.1 us
    pallas_call x2, Pallas kernels, sum_delays(): pl.pallas_call(functools.partial(sum_kernel, last), grid=(subs,), in_spec...  30.9 us
    all_to_all x2, waiting for transfers between devices, per_device(): held = lax.all_to_all(formed, AXES, 0, 0)  17.8 us
    all_to_all x2, starting transfers between devices, per_device(): held = lax.all_to_all(formed, AXES, 0, 0)  17.2 us
    all_to_all x1, blocking collectives, per_device(): parts = lax.all_to_all(total.reshape(shards, samples, 8, NDM), 'tm', 0, 0)  12.7 us
    pallas_call x1, Pallas kernels, route(): pl.pallas_call(route_kernel, in_specs=[whole, whole, whole], out_specs=[w...  6.47 us
  transfers between devices with their start and end apart: 2, of which 2 were waited for; matrix products, arithmetic and copies ran while one was open for 2% of the time, Pallas kernels for 27%

profile of v2, /device:TPU:1, one launch (start us, length us, event | category | flops | bytes accessed | tf_op | source)
XLA Modules:
  0.0 127.0 jit_solution(6600556545143889868)
XLA Ops:
  0.0 6.5 %route.1 = (bf16[8,256,512]{2,1,0:T(8,128)(2,1)}, bf16[8,512,256]{2,1,0:T(8,128)(2,1)}, bf16[1024,1024]{1,0:T(8,128)(2,1)}, s32[1]{0:T(128)}) custom-call(s32[1,2048]{1,0:T(1,128)} %bitcast.10, s32[1,1024]{1,0:T(1,128)} %bitcast.13, bf16[256,256]{1,0:T(8,128)(2,1)} %constant.4.clone.table_ref), custom_call_target="tpu_custom_call" | custom-call | tf_op jit(solution)/shard_map/route/pallas_call | solution.py:83
  6.5 19.6 %form_beams.3 = s16[128,56,128]{2,1,0:T(8,128)(2,1)} custom-call(bf16[512,3,2,2048]{3,2,1,0:T(2,128)(2,1)} %volt_ref.3, s32[1,2048]{1,0:T(1,128)} %bitcast.11, bf16[256,256]{1,0:T(8,128)(2,1)} %constant.4.clone.table_ref, bf16[8,256,512]{2,1,0:T(8,128)(2,1)} %get-tuple-element.9.first_ref, bf16[8,512,256]{2,1,0:T(8,128)(2,1)} %get-tuple-element.10.second_ref, ...), custom_call_target="tpu_custom_call" | custom-call | flops 9663676416 | bytes 12582912 | tf_op jit(solution)/shard_map/form_beams/pallas_call | solution.py:209
  26.1 11.5 %all-to-all-start.1 = ((s16[128,56,128]{2,1,0:T(8,128)(2,1)}), s16[128,56,128]{2,1,0:T(8,128)(2,1)S(1)}, u32[]{:S(2)}, u32[]{:S(2)}) async-start(s16[128,56,128]{2,1,0:T(8,128)(2,1)} %form_beams.3), calls=%async_computation.1 | async-start | bytes 3670016 | tf_op jit(solution)/shard_map/all_to_all | solution.py:317
  37.7 19.4 %form_beams.2 = s16[128,56,128]{2,1,0:T(8,128)(2,1)} custom-call(bf16[512,3,2,2048]{3,2,1,0:T(2,128)(2,1)} %volt_ref.3, s32[1,2048]{1,0:T(1,128)} %bitcast.12, bf16[256,256]{1,0:T(8,128)(2,1)} %constant.4.clone.table_ref, bf16[8,256,512]{2,1,0:T(8,128)(2,1)} %get-tuple-element.9.first_ref, bf16[8,512,256]{2,1,0:T(8,128)(2,1)} %get-tuple-element.10.second_ref, ...), custom_call_target="tpu_custom_call" | custom-call | flops 9663676416 | bytes 12582912 | tf_op jit(solution)/shard_map/form_beams/pallas_call | solution.py:209
  57.1 0.0 copy-start.1
  57.1 0.0 copy-start.2
  57.1 8.0 %all-to-all-done.1.held_ref = s16[128,56,128]{2,1,0:T(8,128)(2,1)S(1)} async-done(((s16[128,56,128]{2,1,0:T(8,128)(2,1)}), s16[128,56,128]{2,1,0:T(8,128)(2,1)S(1)}, u32[]{:S(2)}, u32[]{:S(2)}) %all-to-all-start.1) | async-done | bytes 1835040 | tf_op jit(solution)/shard_map/all_to_all | solution.py:317
  65.1 0.0 copy-start
  65.1 5.7 %all-to-all-start = ((s16[128,56,128]{2,1,0:T(8,128)(2,1)}), s16[128,56,128]{2,1,0:T(8,128)(2,1)}, u32[]{:S(2)}, u32[]{:S(2)}) async-start(s16[128,56,128]{2,1,0:T(8,128)(2,1)} %form_beams.2), calls=%async_computation | async-start | bytes 3670016 | tf_op jit(solution)/shard_map/all_to_all | solution.py:317
  70.8 0.0 copy-done.1
  70.9 0.0 copy-done.2
  70.9 0.6 convert_element_type.7
  71.5 0.7 fusion
  72.1 0.8 broadcast_in_dim.3.before_ref
  72.9 0.0 copy-done
  72.9 15.4 %sum_delays.2.before_ref = f32[192,512]{1,0:T(8,128)} custom-call(s16[128,56,128]{2,1,0:T(8,128)(2,1)} %copy-done, f32[16,1,256]{2,1,0:T(1,128)} %get-tuple-element.13.lag_ref, f32[1,512]{1,0:T(1,128)} %bitcast.14, f32[192,512]{1,0:T(8,128)} %broadcast_in_dim.3.before_ref), custom_call_target="tpu_custom_call" | custom-call | flops 5637144576 | bytes 1572864 | tf_op jit(solution)/shard_map/sum_delays/pallas_call | solution.py:283
  88.4 9.8 %all-to-all-done.held_ref = s16[128,56,128]{2,1,0:T(8,128)(2,1)} async-done(((s16[128,56,128]{2,1,0:T(8,128)(2,1)}), s16[128,56,128]{2,1,0:T(8,128)(2,1)}, u32[]{:S(2)}, u32[]{:S(2)}) %all-to-all-start) | async-done | bytes 1835040 | tf_op jit(solution)/shard_map/all_to_all | solution.py:317
  98.1 15.5 %sum_delays.3 = f32[192,512]{1,0:T(8,128)} custom-call(s16[128,56,128]{2,1,0:T(8,128)(2,1)} %all-to-all-done.held_ref, f32[16,1,256]{2,1,0:T(1,128)} %get-tuple-element.14.lag_ref, f32[1,512]{1,0:T(1,128)} %bitcast.15, f32[192,512]{1,0:T(8,128)} %sum_delays.2.before_ref), custom_call_target="tpu_custom_call" | custom-call | flops 5637144576 | bytes 1572864 | tf_op jit(solution)/shard_map/sum_delays/pallas_call | solution.py:283
  113.6 12.7 %all_to_all.15 = f32[8,3,8,512]{3,2,1,0:T(8,128)S(1)} all-to-all(f32[8,3,8,512]{3,2,1,0:T(8,128)} %bitcast.9), channel_id=1, replica_groups=mesh['sub'=16,'tm'=8] {'tm'}, dimensions={0} | all-to-all | bytes 786432 | tf_op jit(solution)/shard_map/all_to_all | solution.py:319
  126.3 0.8 copy_bitcast_fusion
  (2 shorter events, 0.0 us)
Async XLA Ops:
  26.1 39.0 %all-to-all-start.1 = ((s16[128,56,128]{2,1,0:T(8,128)(2,1)}), s16[128,56,128]{2,1,0:T(8,128)(2,1)S(1)}, u32[]{:S(2)}, u32[]{:S(2)}) async-start(s16[128,56,128]{2,1,0:T(8,128)(2,1)} %form_beams.3), calls=%async_computation.1 | async-start | bytes 3670016 | tf_op jit(solution)/shard_map/all_to_all | solution.py:317
  57.1 13.7 %copy-start.1 = (s32[8192]{0:T(1024)S(1)}, s32[8192]{0:T(1024)}, u32[]{:S(2)}) copy-start(s32[8192]{0:T(1024)} %param.8) | copy-start | bytes 98308
  57.1 13.8 %copy-start.2 = (s32[512]{0:T(512)S(1)}, s32[512]{0:T(512)}, u32[]{:S(2)}) copy-start(s32[512]{0:T(512)} %param.9) | copy-start | bytes 6148
  65.1 7.8 %copy-start = (s16[128,56,128]{2,1,0:T(8,128)(2,1)}, s16[128,56,128]{2,1,0:T(8,128)(2,1)S(1)}, u32[]{:S(2)}) copy-start(s16[128,56,128]{2,1,0:T(8,128)(2,1)S(1)} %all-to-all-done.1.held_ref) | copy-start | bytes 5505028
  65.1 33.0 %all-to-all-start = ((s16[128,56,128]{2,1,0:T(8,128)(2,1)}), s16[128,56,128]{2,1,0:T(8,128)(2,1)}, u32[]{:S(2)}, u32[]{:S(2)}) async-start(s16[128,56,128]{2,1,0:T(8,128)(2,1)} %form_beams.2), calls=%async_computation | async-start | bytes 3670016 | tf_op jit(solution)/shard_map/all_to_all | solution.py:317

commit v3 on v2

--- a/solution.py
+++ b/solution.py
@@ -24,6 +24,9 @@
 LEVELS = 65535.0
 HALF = 32768.0
 STEPS = 256.0
+ROUND = 12582912.0
+SLAB = 32
+TOGETHER = 8
 GROUPS = 8
 ROOM = 64
 SAMPLE_ROWS = 48
@@ -96,7 +99,8 @@
 
 
 def form_kernel(
-    volt_ref, feed_ref, table_ref, first_ref, second_ref, pick_ref, deepest_ref, out_ref, grid_ref, unit_ref
+    volt_ref, feed_ref, table_ref, first_ref, second_ref, pick_ref, deepest_ref, out_ref,
+    grid_ref, unit_ref, power_ref, peak_ref, high_ref, low_ref,
 ):
     chans = volt_ref.shape[0]
     half = NS // 2
@@ -141,14 +145,14 @@
             grid_ref[2 * d] = wave[:, :half]
             grid_ref[2 * d + 1] = wave[:, half:]
 
-    edge = lax.broadcasted_iota(jnp.int32, (chans, half), 1) == 0
-
-    def west(p, part):
+    edge = lax.broadcasted_iota(jnp.int32, (SLAB, half), 1) == 0
+
+    def west(p, part, at):
         re, im = [], []
         for y in range(CYL):
             tile = 2 * (p * CYL + y) + part
-            re.append(grid_ref[tile, pl.ds(0, chans, stride=2), :])
-            im.append(grid_ref[tile, pl.ds(1, chans, stride=2), :])
+            re.append(grid_ref[tile, pl.ds(2 * at, SLAB, stride=2), :])
+            im.append(grid_ref[tile, pl.ds(2 * at + 1, SLAB, stride=2), :])
         a_re, a_im = re[0] + re[2], im[0] + im[2]
         b_re, b_im = re[0] - re[2], im[0] - im[2]
         c_re, c_im = re[1] + re[3], im[1] + im[3]
@@ -160,31 +164,43 @@
             (b_re - d_im, b_im + d_re),
         ]
 
-    power = [None] * (2 * CYL)
-    for p in range(POL):
-        for e, ((c_re, c_im), (s_re, s_im)) in enumerate(zip(west(p, 0), west(p, 1))):
-            t_re, t_im = jnp.where(edge, 0.0, s_re), jnp.where(edge, 0.0, s_im)
-            u_re, u_im = c_re + t_im, c_im - t_re
-            v_re, v_im = jnp.where(edge, s_re, c_re - t_im), jnp.where(edge, s_im, c_im + t_re)
-            for at, (w_re, w_im) in ((2 * e, (u_re, u_im)), (2 * e + 1, (v_re, v_im))):
-                square = w_re * w_re + w_im * w_im
-                power[at] = square if power[at] is None else power[at] + square
-    power = jnp.concatenate(power, axis=1)
-    most = jnp.maximum(jnp.max(power, axis=1, keepdims=True), 1e-30)
+    for at in range(0, chans, SLAB):
+        power = [None] * (2 * CYL)
+        for p in range(POL):
+            for e, ((c_re, c_im), (s_re, s_im)) in enumerate(zip(west(p, 0, at), west(p, 1, at))):
+                t_re, t_im = jnp.where(edge, 0.0, s_re), jnp.where(edge, 0.0, s_im)
+                u_re, u_im = c_re + t_im, c_im - t_re
+                v_re, v_im = jnp.where(edge, s_re, c_re - t_im), jnp.where(edge, s_im, c_im + t_re)
+                for i, (w_re, w_im) in ((2 * e, (u_re, u_im)), (2 * e + 1, (v_re, v_im))):
+                    square = w_re * w_re + w_im * w_im
+                    power[i] = square if power[i] is None else power[i] + square
+        peak = power[0]
+        for i, square in enumerate(power):
+            power_ref[at : at + SLAB, i * half : (i + 1) * half] = square
+            peak = jnp.maximum(peak, square)
+        peak_ref[at : at + SLAB] = peak
+    most = jnp.maximum(jnp.max(peak_ref[...], axis=1, keepdims=True), 1e-30)
     level = jnp.ceil(jnp.log2(most) * STEPS) + 1.0
     scale = LEVELS * jnp.exp2(level * (-1.0 / STEPS))
-    code = jnp.floor(power * scale + 0.5)
-    high = jnp.floor(code * (1.0 / 256.0)) * 256.0
-    low = (code - high).astype(jnp.bfloat16)
-    total = None
-    for piece in (high.astype(jnp.bfloat16), low):
-        part = lax.dot_general(
-            pick_ref[...], piece, (((1,), (1,)), ((), ())), preferred_element_type=jnp.float32
+    for at in range(0, chans, SLAB):
+        factor = jnp.broadcast_to(scale[at : at + SLAB], (SLAB, half))
+        for i in range(2 * CYL):
+            lanes = slice(i * half, (i + 1) * half)
+            code = (power_ref[at : at + SLAB, lanes] * factor + (ROUND - HALF)) - ROUND
+            high = ((code * (1.0 / 256.0) - (0.5 - 1.0 / 512.0) + ROUND) - ROUND) * 256.0
+            high_ref[at : at + SLAB, lanes] = high.astype(jnp.bfloat16)
+            low_ref[at : at + SLAB, lanes] = (code - high).astype(jnp.bfloat16)
+    parts = [
+        lax.dot_general(
+            pick_ref[...], ref[...], (((1,), (1,)), ((), ())), preferred_element_type=jnp.float32
         )
-        total = part if total is None else total + part
-    total = (total - HALF).reshape(BEAMS // 8, 8, chans)
-    both = jnp.concatenate([total[:, :, : chans // 2], total[:, :, chans // 2 :]], axis=1)
-    out_ref[:, pl.ds(pl.multiple_of(16 * t, 16), 16), :] = both.astype(jnp.int32).astype(jnp.int16)
+        for ref in (high_ref, low_ref)
+    ]
+    for group in range(BEAMS // 8):
+        rows = slice(8 * group, 8 * group + 8)
+        total = parts[0][rows] + parts[1][rows]
+        both = jnp.concatenate([total[:, : chans // 2], total[:, chans // 2 :]], axis=0)
+        out_ref[group, pl.ds(pl.multiple_of(16 * t, 16), 16), :] = both.astype(jnp.int32).astype(jnp.int16)
     levels = jnp.transpose(jnp.broadcast_to(level, (chans, 128)))[:1]
     unit_ref[pl.ds(2 * t, 1), :] = levels[:, : chans // 2]
     unit_ref[pl.ds(2 * t + 1, 1), :] = levels[:, chans // 2 :]
@@ -223,6 +239,10 @@
         scratch_shapes=[
             pltpu.VMEM((FEEDS // 128, 2 * block, 128), jnp.float32),
             pltpu.VMEM((8, block // 2), jnp.float32),
+            pltpu.VMEM((block, BEAMS), jnp.float32),
+            pltpu.VMEM((block, 128), jnp.float32),
+            pltpu.VMEM((block, BEAMS), jnp.bfloat16),
+            pltpu.VMEM((block, BEAMS), jnp.bfloat16),
         ],
         compiler_params=pltpu.CompilerParams(vmem_limit_bytes=56 * 2**20),
         cost_estimate=pl.CostEstimate(
@@ -234,90 +254,164 @@
     )(voltages, slot_feed, table, first, second, pick, deepest)
 
 
-def sum_kernel(last, held_ref, lag_ref, trial_ref, before_ref, out_ref):
-    chans = 2 * held_ref.shape[-1]
-    step = pl.program_id(0)
-
-    @pl.when(step == 0)
-    def _():
-        out_ref[...] = before_ref[...]
-
-    shards = held_ref.shape[0]
-    code = held_ref[:, :SAMPLE_ROWS, :].reshape(TIME, 16, chans // 2).astype(jnp.float32) + HALF
-    code = jnp.concatenate([code[:, :8], code[:, 8:]], axis=2)
-    level = held_ref[:, SAMPLE_ROWS:, :].astype(jnp.float32)
-    unit = jnp.exp2(level[:, :8] * (1.0 / STEPS)) * (0.25 / LEVELS)
+def normal_rows(held_ref, at):
+    shards = held_ref.shape[0] // TOGETHER
+    samples = TIME // shards
+    half = held_ref.shape[-1]
     parts = []
     for shard in range(shards):
-        for t in range(TIME // shards):
-            row = jnp.concatenate(
-                [unit[shard, 2 * t : 2 * t + 1], unit[shard, 2 * t + 1 : 2 * t + 2]], axis=1
-            )
-            parts.append(code[shard * (TIME // shards) + t] * row)
-    held = jnp.stack(parts)
-    average = jnp.sum(held, axis=0) / TIME
-    normal = (held - average[None]).reshape(TIME * 8, chans).astype(jnp.bfloat16)
-    lag = jnp.transpose(jnp.broadcast_to(lag_ref[0], (8, chans)))[:, :1]
-    product = lag * trial_ref[...]
-    delay = jnp.floor(product * (1.0 / QUANT)).astype(jnp.bfloat16)
+        block = held_ref.at[at * shards + shard]
+        level = block[SAMPLE_ROWS:, :].astype(jnp.float32)
+        unit = jnp.exp2(level * (1.0 / STEPS)) * (0.25 / LEVELS)
+        for t in range(samples):
+            code = block[16 * t : 16 * t + 16, :].astype(jnp.float32) + HALF
+            ends = [
+                code[8 * h : 8 * h + 8] * unit[2 * t + h : 2 * t + h + 1] for h in range(2)
+            ]
+            parts.append(jnp.concatenate(ends, axis=1))
+    average = functools.reduce(jnp.add, parts) / TIME
+    rows = [
+        jnp.concatenate([parts[i] - average, parts[i + 1] - average], axis=0).astype(jnp.bfloat16)
+        for i in range(0, TIME, 2)
+    ]
+    return jnp.concatenate(rows, axis=0)
+
+
+def add_delayed(held_ref, lag_ref, trial_ref, total_ref):
+    normals, delays = [], []
+    for at in range(TOGETHER):
+        normals.append(normal_rows(held_ref, at))
+        lag = column_of(lag_ref[at])
+        delays.append(jnp.floor(lag * trial_ref[...] * (1.0 / QUANT)).astype(jnp.bfloat16))
+    normal = jnp.concatenate(normals, axis=1)
+    delay = jnp.concatenate(delays, axis=0)
     one, zero = jnp.ones((), jnp.bfloat16), jnp.zeros((), jnp.bfloat16)
     for k in range(MAXD + 1):
         onehot = jnp.where(delay == jnp.bfloat16(k), one, zero)
         keep = TIME * 8 - 8 * k
         rows = -(-keep // 16) * 16
         part = jnp.dot(normal[:rows], onehot, preferred_element_type=jnp.float32)
-        out_ref[8 * k :, :] += part[:keep]
-
-    if last:
-
-        @pl.when(step == pl.num_programs(0) - 1)
-        def _():
-            out_ref[...] = out_ref[...] * (1.0 / math.sqrt(CHANNELS))
-
-
-def sum_delays(held, lags, trials, before, last):
+        total_ref[8 * k :, :] += part[:keep]
+
+
+def sum_kernel(held_ref, lag_ref, trial_ref, total_ref):
+    @pl.when(pl.program_id(0) == 0)
+    def _():
+        total_ref[...] = jnp.zeros_like(total_ref)
+
+    add_delayed(held_ref, lag_ref, trial_ref, total_ref)
+
+
+def share_kernel(
+    held_ref, lag_ref, trial_ref, before_ref, out_ref, total_ref, landed_ref, send_sem, recv_sem
+):
+    shards, rows = landed_ref.shape[0], landed_ref.shape[1]
+    step = pl.program_id(0)
+    me = lax.axis_index("tm")
+    barrier = pltpu.get_barrier_semaphore()
+
+    def device(other):
+        return (lax.axis_index("sub"), other)
+
+    def copy(i):
+        other = lax.rem(me + i, shards)
+        return pltpu.make_async_remote_copy(
+            src_ref=total_ref.at[pl.ds(pl.multiple_of(other * rows, 8), rows), :],
+            dst_ref=landed_ref.at[me],
+            send_sem=send_sem.at[i],
+            recv_sem=recv_sem.at[i],
+            device_id=device(other),
+            device_id_type=pl.DeviceIdType.MESH,
+        )
+
+    @pl.when(step == 0)
+    def _():
+        for i in range(1, shards):
+            pl.semaphore_signal(
+                barrier, inc=1, device_id=device(lax.rem(me + i, shards)), device_id_type=pl.DeviceIdType.MESH
+            )
+        total_ref[...] = before_ref[...]
+
+    add_delayed(held_ref, lag_ref, trial_ref, total_ref)
+
+    @pl.when(step == pl.num_programs(0) - 1)
+    def _():
+        pl.semaphore_wait(barrier, shards - 1)
+        copies = [copy(i) for i in range(1, shards)]
+        for each in copies:
+            each.start()
+        landed_ref[me] = total_ref[pl.ds(pl.multiple_of(me * rows, 8), rows), :]
+        for each in copies:
+            each.wait()
+        scale = 1.0 / math.sqrt(CHANNELS)
+        for shard in range(shards):
+            for t in range(rows // 8):
+                out_ref[t, 8 * shard : 8 * shard + 8, :] = landed_ref[shard, 8 * t : 8 * t + 8, :] * scale
+
+
+def sum_delays(held, lags, trials, before):
     chans = 2 * held.shape[-1]
     subs = lags.shape[0]
     shards = held.shape[0] // subs
     rows = TIME * 8
+    whole = pl.BlockSpec(memory_space=pltpu.VMEM)
+    in_specs = [
+        pl.BlockSpec((TOGETHER * shards, ROWS, chans // 2), lambda s: (s, 0, 0)),
+        pl.BlockSpec((TOGETHER, 1, chans), lambda s: (s, 0, 0)),
+        whole,
+    ]
+    cost = pl.CostEstimate(
+        flops=2 * subs * chans * rows * NDM * 7,
+        bytes_accessed=subs * chans * rows * 2,
+        transcendentals=0,
+    )
+    if before is None:
+        return pl.pallas_call(
+            sum_kernel,
+            grid=(subs // TOGETHER,),
+            in_specs=in_specs,
+            out_specs=pl.BlockSpec((rows, NDM), lambda s: (0, 0)),
+            out_shape=jax.ShapeDtypeStruct((rows, NDM), jnp.float32),
+            compiler_params=pltpu.CompilerParams(vmem_limit_bytes=56 * 2**20),
+            cost_estimate=cost,
+            name="sum_delays",
+        )(held, lags, trials)
+    samples = TIME // shards
     return pl.pallas_call(
-        functools.partial(sum_kernel, last),
-        grid=(subs,),
-        in_specs=[
-            pl.BlockSpec((shards, ROWS, chans // 2), lambda s: (s, 0, 0)),
-            pl.BlockSpec((1, 1, chans), lambda s: (s, 0, 0)),
-            pl.BlockSpec(memory_space=pltpu.VMEM),
-            pl.BlockSpec(memory_space=pltpu.VMEM),
+        share_kernel,
+        grid=(subs // TOGETHER,),
+        in_specs=in_specs + [whole],
+        out_specs=pl.BlockSpec((samples, 8 * shards, NDM), lambda s: (0, 0, 0)),
+        out_shape=jax.ShapeDtypeStruct((samples, 8 * shards, NDM), jnp.float32),
+        scratch_shapes=[
+            pltpu.VMEM((rows, NDM), jnp.float32),
+            pltpu.VMEM((shards, rows // shards, NDM), jnp.float32),
+            pltpu.SemaphoreType.DMA((shards,)),
+            pltpu.SemaphoreType.DMA((shards,)),
         ],
-        out_specs=pl.BlockSpec((rows, NDM), lambda s: (0, 0)),
-        out_shape=jax.ShapeDtypeStruct((rows, NDM), jnp.float32),
-        compiler_params=pltpu.CompilerParams(vmem_limit_bytes=56 * 2**20),
-        cost_estimate=pl.CostEstimate(
-            flops=2 * subs * chans * rows * NDM * 7,
-            bytes_accessed=subs * chans * rows * 2,
-            transcendentals=0,
+        compiler_params=pltpu.CompilerParams(
+            vmem_limit_bytes=56 * 2**20, collective_id=0, has_side_effects=True
         ),
-        name="sum_delays",
+        cost_estimate=cost,
+        name="sum_and_share",
     )(held, lags, trials, before)
 
 
 def per_device(voltages, slot_feed, chan_lag, trial_dm, beam_order):
-    samples = voltages.shape[1]
-    subs, shards = lax.axis_size("sub"), lax.axis_size("tm")
+    subs = lax.axis_size("sub")
     table = jnp.asarray(half_table())
     lags = chan_lag.astype(jnp.float32).reshape(subs, CHUNKS, -1)
     trials = trial_dm.astype(jnp.float32).reshape(1, NDM)
     feeds = slot_feed.reshape(1, FEEDS)
     order = beam_order.reshape(1, BEAMS)
     chans = voltages.shape[0] // CHUNKS
-    total = jnp.zeros((TIME * 8, NDM), jnp.float32)
+    total = None
     first, second, pick, deepest = route(feeds, order, table)
     for chunk in range(CHUNKS):
         formed = form_beams(voltages, feeds, table, first, second, pick, deepest, chunk, chans)
         held = lax.all_to_all(formed, AXES, 0, 0)
-        total = sum_delays(held, lags[:, chunk : chunk + 1], trials, total, chunk == CHUNKS - 1)
-    parts = lax.all_to_all(total.reshape(shards, samples, 8, NDM), "tm", 0, 0)
-    return parts.transpose(0, 2, 1, 3).reshape(shards * 8, samples, NDM)
+        total = sum_delays(held, lags[:, chunk : chunk + 1], trials, total)
+    return total.transpose(1, 0, 2)
 
 
 def solution(mesh):

time: 128 us -> 116 us (0.906)
  blocking collectives: 12.7 us -> 0 us
  waiting for transfers between devices: 17.8 us -> 23.9 us
  Pallas kernels: 76.4 us -> 71.4 us
    all_to_all x1 -> x0, blocking collectives: 12.7 us -> none  [per_device(): parts = lax.all_to_all(total.reshape(shards, samples, 8, NDM), 'tm', 0, 0)]
    pallas_call x2, Pallas kernels: 30.9 us -> 24.8 us  [the longest x1 15.2 us: sum_delays(): pl.pallas_call(share_kernel, grid=(subs // TOGETHER,), in_specs=in_specs...]
    all_to_all x2, waiting for transfers between devices: 17.8 us -> 23.9 us  [per_device(): held = lax.all_to_all(formed, AXES, 0, 0)]
    unnamed x6 -> x7, local copies, waits for them, and re-layouts: 0.01 us -> 1.78 us
  transfers between devices with their start and end apart: 2 -> 2, of which waited for: 2 -> 2; matrix products, arithmetic and copies ran while one was open for 2% -> 1% of each run, Pallas kernels for 27% -> 26%
where the time goes in v3:
time: 116 us
  Pallas kernels  71.4 us (62%)
  waiting for transfers between devices  23.9 us (21%)
  starting transfers between devices  17.2 us (15%)
  local copies, waits for them, and re-layouts  2.45 us (2%)
    pallas_call x2, Pallas kernels, form_beams(): pl.pallas_call(form_kernel, grid=(steps, samples), in_specs=[pl.BlockSpec...  40.1 us
    all_to_all x2, waiting for transfers between devices, per_device(): held = lax.all_to_all(formed, AXES, 0, 0)  23.9 us
    all_to_all x2, starting transfers between devices, per_device(): held = lax.all_to_all(formed, AXES, 0, 0)  17.2 us
    pallas_call x1, Pallas kernels, sum_delays(): pl.pallas_call(share_kernel, grid=(subs // TOGETHER,), in_specs=in_specs...  15.2 us
    pallas_call x1, Pallas kernels, sum_delays(): pl.pallas_call(sum_kernel, grid=(subs // TOGETHER,), in_specs=in_specs, o...  9.65 us
    pallas_call x1, Pallas kernels, route(): pl.pallas_call(route_kernel, in_specs=[whole, whole, whole], out_specs=[w...  6.47 us
  transfers between devices with their start and end apart: 2, of which 2 were waited for; matrix products, arithmetic and copies ran while one was open for 1% of the time, Pallas kernels for 26%

profile of v3, /device:TPU:1, one launch (start us, length us, event | category | flops | bytes accessed | tf_op | source)
XLA Modules:
  0.0 115.6 jit_solution(17033203886954634572)
XLA Ops:
  0.0 6.5 %route.1 = (bf16[8,256,512]{2,1,0:T(8,128)(2,1)}, bf16[8,512,256]{2,1,0:T(8,128)(2,1)}, bf16[1024,1024]{1,0:T(8,128)(2,1)}, s32[1]{0:T(128)}) custom-call(s32[1,2048]{1,0:T(1,128)} %bitcast.5, s32[1,1024]{1,0:T(1,128)} %bitcast.8, bf16[256,256]{1,0:T(8,128)(2,1)} %constant.2.clone.table_ref), custom_call_target="tpu_custom_call" | custom-call | tf_op jit(solution)/shard_map/route/pallas_call | solution.py:86
  6.5 20.2 %form_beams.3 = s16[128,56,128]{2,1,0:T(8,128)(2,1)} custom-call(bf16[512,3,2,2048]{3,2,1,0:T(2,128)(2,1)} %volt_ref.3, s32[1,2048]{1,0:T(1,128)} %bitcast.6, bf16[256,256]{1,0:T(8,128)(2,1)} %constant.2.clone.table_ref, bf16[8,256,512]{2,1,0:T(8,128)(2,1)} %get-tuple-element.9.first_ref, bf16[8,512,256]{2,1,0:T(8,128)(2,1)} %get-tuple-element.10.second_ref, ...), custom_call_target="tpu_custom_call" | custom-call | flops 9663676416 | bytes 12582912 | tf_op jit(solution)/shard_map/form_beams/pallas_call | solution.py:225
  26.7 11.5 %all-to-all-start.1 = ((s16[128,56,128]{2,1,0:T(8,128)(2,1)}), s16[128,56,128]{2,1,0:T(8,128)(2,1)S(1)}, u32[]{:S(2)}, u32[]{:S(2)}) async-start(s16[128,56,128]{2,1,0:T(8,128)(2,1)} %form_beams.3), calls=%async_computation.1 | async-start | bytes 3670016 | tf_op jit(solution)/shard_map/all_to_all | solution.py:412
  38.2 19.9 %form_beams.2 = s16[128,56,128]{2,1,0:T(8,128)(2,1)} custom-call(bf16[512,3,2,2048]{3,2,1,0:T(2,128)(2,1)} %volt_ref.3, s32[1,2048]{1,0:T(1,128)} %bitcast.7, bf16[256,256]{1,0:T(8,128)(2,1)} %constant.2.clone.table_ref, bf16[8,256,512]{2,1,0:T(8,128)(2,1)} %get-tuple-element.9.first_ref, bf16[8,512,256]{2,1,0:T(8,128)(2,1)} %get-tuple-element.10.second_ref, ...), custom_call_target="tpu_custom_call" | custom-call | flops 9663676416 | bytes 12582912 | tf_op jit(solution)/shard_map/form_beams/pallas_call | solution.py:225
  58.1 0.0 copy-start.1
  58.1 0.0 copy-start.2
  58.1 7.5 %all-to-all-done.1.held_ref = s16[128,56,128]{2,1,0:T(8,128)(2,1)S(1)} async-done(((s16[128,56,128]{2,1,0:T(8,128)(2,1)}), s16[128,56,128]{2,1,0:T(8,128)(2,1)S(1)}, u32[]{:S(2)}, u32[]{:S(2)}) %all-to-all-start.1) | async-done | bytes 1835040 | tf_op jit(solution)/shard_map/all_to_all | solution.py:412
  65.6 0.0 copy-start
  65.6 5.7 %all-to-all-start = ((s16[128,56,128]{2,1,0:T(8,128)(2,1)}), s16[128,56,128]{2,1,0:T(8,128)(2,1)}, u32[]{:S(2)}, u32[]{:S(2)}) async-start(s16[128,56,128]{2,1,0:T(8,128)(2,1)} %form_beams.2), calls=%async_computation | async-start | bytes 3670016 | tf_op jit(solution)/shard_map/all_to_all | solution.py:412
  71.3 0.0 copy-done.1
  71.4 0.0 copy-done.2
  71.4 0.6 convert_element_type.7
  72.0 0.6 fusion
  72.6 0.0 copy-done
  72.6 9.6 %sum_delays.1.before_ref = f32[192,512]{1,0:T(8,128)} custom-call(s16[128,56,128]{2,1,0:T(8,128)(2,1)} %copy-done, f32[16,1,256]{2,1,0:T(1,128)} %get-tuple-element.13.lag_ref, f32[1,512]{1,0:T(1,128)} %bitcast.9), custom_call_target="tpu_custom_call" | custom-call | flops 5637144576 | bytes 1572864 | tf_op jit(solution)/shard_map/sum_delays/pallas_call | solution.py:369
  82.3 16.3 %all-to-all-done.held_ref = s16[128,56,128]{2,1,0:T(8,128)(2,1)} async-done(((s16[128,56,128]{2,1,0:T(8,128)(2,1)}), s16[128,56,128]{2,1,0:T(8,128)(2,1)}, u32[]{:S(2)}, u32[]{:S(2)}) %all-to-all-start) | async-done | bytes 1835040 | tf_op jit(solution)/shard_map/all_to_all | solution.py:412
  98.6 15.2 %sum_and_share.1 = f32[3,64,512]{2,1,0:T(8,128)} custom-call(s16[128,56,128]{2,1,0:T(8,128)(2,1)} %all-to-all-done.held_ref, f32[16,1,256]{2,1,0:T(1,128)} %get-tuple-element.14.lag_ref, f32[1,512]{1,0:T(1,128)} %bitcast.10, f32[192,512]{1,0:T(8,128)} %sum_delays.1.before_ref), custom_call_target="tpu_custom_call" | custom-call | flops 5637144576 | bytes 1572864 | tf_op jit(solution)/shard_map/sum_and_share/pallas_call | solution.py:380
  113.8 1.8 %copy.8 = f32[64,3,512]{2,0,1:T(8,128)} copy(f32[64,3,512]{2,0,1:T(8,128)} %bitcast.4) | data formatting | bytes 786432
  (2 shorter events, 0.0 us)
Async XLA Ops:
  26.7 39.0 %all-to-all-start.1 = ((s16[128,56,128]{2,1,0:T(8,128)(2,1)}), s16[128,56,128]{2,1,0:T(8,128)(2,1)S(1)}, u32[]{:S(2)}, u32[]{:S(2)}) async-start(s16[128,56,128]{2,1,0:T(8,128)(2,1)} %form_beams.3), calls=%async_computation.1 | async-start | bytes 3670016 | tf_op jit(solution)/shard_map/all_to_all | solution.py:412
  58.1 13.2 %copy-start.1 = (s32[8192]{0:T(1024)S(1)}, s32[8192]{0:T(1024)}, u32[]{:S(2)}) copy-start(s32[8192]{0:T(1024)} %param.8) | copy-start | bytes 98308
  58.1 13.3 %copy-start.2 = (s32[512]{0:T(512)S(1)}, s32[512]{0:T(512)}, u32[]{:S(2)}) copy-start(s32[512]{0:T(512)} %param.9) | copy-start | bytes 6148
  65.6 7.0 %copy-start = (s16[128,56,128]{2,1,0:T(8,128)(2,1)}, s16[128,56,128]{2,1,0:T(8,128)(2,1)S(1)}, u32[]{:S(2)}) copy-start(s16[128,56,128]{2,1,0:T(8,128)(2,1)S(1)} %all-to-all-done.1.held_ref) | copy-start | bytes 5505028
  65.6 33.0 %all-to-all-start = ((s16[128,56,128]{2,1,0:T(8,128)(2,1)}), s16[128,56,128]{2,1,0:T(8,128)(2,1)}, u32[]{:S(2)}, u32[]{:S(2)}) async-start(s16[128,56,128]{2,1,0:T(8,128)(2,1)} %form_beams.2), calls=%async_computation | async-start | bytes 3670016 | tf_op jit(solution)/shard_map/all_to_all | solution.py:412

commit v4 on v3

--- a/solution.py
+++ b/solution.py
@@ -25,7 +25,6 @@
 HALF = 32768.0
 STEPS = 256.0
 ROUND = 12582912.0
-SLAB = 32
 TOGETHER = 8
 GROUPS = 8
 ROOM = 64
@@ -99,8 +98,7 @@
 
 
 def form_kernel(
-    volt_ref, feed_ref, table_ref, first_ref, second_ref, pick_ref, deepest_ref, out_ref,
-    grid_ref, unit_ref, power_ref, peak_ref, high_ref, low_ref,
+    volt_ref, feed_ref, table_ref, first_ref, second_ref, pick_ref, deepest_ref, out_ref, grid_ref, unit_ref
 ):
     chans = volt_ref.shape[0]
     half = NS // 2
@@ -109,6 +107,56 @@
     @pl.when(t == 0)
     def _():
         unit_ref[...] = jnp.zeros_like(unit_ref)
+
+    def finish():
+        edge = lax.broadcasted_iota(jnp.int32, (chans, half), 1) == 0
+
+        def west(p, part):
+            re, im = [], []
+            for y in range(CYL):
+                tile = 2 * (p * CYL + y) + part
+                re.append(grid_ref[tile, pl.ds(0, chans, stride=2), :])
+                im.append(grid_ref[tile, pl.ds(1, chans, stride=2), :])
+            a_re, a_im = re[0] + re[2], im[0] + im[2]
+            b_re, b_im = re[0] - re[2], im[0] - im[2]
+            c_re, c_im = re[1] + re[3], im[1] + im[3]
+            d_re, d_im = re[1] - re[3], im[1] - im[3]
+            return [
+                (a_re + c_re, a_im + c_im),
+                (b_re + d_im, b_im - d_re),
+                (a_re - c_re, a_im - c_im),
+                (b_re - d_im, b_im + d_re),
+            ]
+
+        power = [None] * (2 * CYL)
+        for p in range(POL):
+            for e, ((c_re, c_im), (s_re, s_im)) in enumerate(zip(west(p, 0), west(p, 1))):
+                t_re, t_im = jnp.where(edge, 0.0, s_re), jnp.where(edge, 0.0, s_im)
+                u_re, u_im = c_re + t_im, c_im - t_re
+                v_re, v_im = jnp.where(edge, s_re, c_re - t_im), jnp.where(edge, s_im, c_im + t_re)
+                for at, (w_re, w_im) in ((2 * e, (u_re, u_im)), (2 * e + 1, (v_re, v_im))):
+                    square = w_re * w_re + w_im * w_im
+                    power[at] = square if power[at] is None else power[at] + square
+        power = jnp.concatenate(power, axis=1)
+        most = jnp.maximum(jnp.max(power, axis=1, keepdims=True), 1e-30)
+        level = jnp.ceil(jnp.log2(most) * STEPS) + 1.0
+        scale = LEVELS * jnp.exp2(level * (-1.0 / STEPS))
+        code = (power * scale + (ROUND - HALF)) - ROUND
+        high = ((code * (1.0 / 256.0) - (0.5 - 1.0 / 512.0) + ROUND) - ROUND) * 256.0
+        low = (code - high).astype(jnp.bfloat16)
+        total = None
+        for piece in (high.astype(jnp.bfloat16), low):
+            part = lax.dot_general(
+                pick_ref[...], piece, (((1,), (1,)), ((), ())), preferred_element_type=jnp.float32
+            )
+            total = part if total is None else total + part
+        total = total.reshape(BEAMS // 8, 8, chans)
+        both = jnp.concatenate([total[:, :, : chans // 2], total[:, :, chans // 2 :]], axis=1)
+        out_ref[:, pl.ds(pl.multiple_of(16 * t, 16), 16), :] = both.astype(jnp.int32).astype(jnp.int16)
+        levels = jnp.transpose(jnp.broadcast_to(level, (chans, 128)))[:1]
+        unit_ref[pl.ds(2 * t, 1), :] = levels[:, : chans // 2]
+        unit_ref[pl.ds(2 * t + 1, 1), :] = levels[:, chans // 2 :]
+
 
     @pl.when(deepest_ref[0] < ROOM)
     def _():
@@ -133,6 +181,7 @@
             )
             grid_ref[2 * d] = wave[:, :half]
             grid_ref[2 * d + 1] = wave[:, half:]
+        finish()
 
     @pl.when(deepest_ref[0] >= ROOM)
     def _():
@@ -144,66 +193,7 @@
             wave = jnp.dot(slots, table_ref[...], preferred_element_type=jnp.float32)
             grid_ref[2 * d] = wave[:, :half]
             grid_ref[2 * d + 1] = wave[:, half:]
-
-    edge = lax.broadcasted_iota(jnp.int32, (SLAB, half), 1) == 0
-
-    def west(p, part, at):
-        re, im = [], []
-        for y in range(CYL):
-            tile = 2 * (p * CYL + y) + part
-            re.append(grid_ref[tile, pl.ds(2 * at, SLAB, stride=2), :])
-            im.append(grid_ref[tile, pl.ds(2 * at + 1, SLAB, stride=2), :])
-        a_re, a_im = re[0] + re[2], im[0] + im[2]
-        b_re, b_im = re[0] - re[2], im[0] - im[2]
-        c_re, c_im = re[1] + re[3], im[1] + im[3]
-        d_re, d_im = re[1] - re[3], im[1] - im[3]
-        return [
-            (a_re + c_re, a_im + c_im),
-            (b_re + d_im, b_im - d_re),
-            (a_re - c_re, a_im - c_im),
-            (b_re - d_im, b_im + d_re),
-        ]
-
-    for at in range(0, chans, SLAB):
-        power = [None] * (2 * CYL)
-        for p in range(POL):
-            for e, ((c_re, c_im), (s_re, s_im)) in enumerate(zip(west(p, 0, at), west(p, 1, at))):
-                t_re, t_im = jnp.where(edge, 0.0, s_re), jnp.where(edge, 0.0, s_im)
-                u_re, u_im = c_re + t_im, c_im - t_re
-                v_re, v_im = jnp.where(edge, s_re, c_re - t_im), jnp.where(edge, s_im, c_im + t_re)
-                for i, (w_re, w_im) in ((2 * e, (u_re, u_im)), (2 * e + 1, (v_re, v_im))):
-                    square = w_re * w_re + w_im * w_im
-                    power[i] = square if power[i] is None else power[i] + square
-        peak = power[0]
-        for i, square in enumerate(power):
-            power_ref[at : at + SLAB, i * half : (i + 1) * half] = square
-            peak = jnp.maximum(peak, square)
-        peak_ref[at : at + SLAB] = peak
-    most = jnp.maximum(jnp.max(peak_ref[...], axis=1, keepdims=True), 1e-30)
-    level = jnp.ceil(jnp.log2(most) * STEPS) + 1.0
-    scale = LEVELS * jnp.exp2(level * (-1.0 / STEPS))
-    for at in range(0, chans, SLAB):
-        factor = jnp.broadcast_to(scale[at : at + SLAB], (SLAB, half))
-        for i in range(2 * CYL):
-            lanes = slice(i * half, (i + 1) * half)
-            code = (power_ref[at : at + SLAB, lanes] * factor + (ROUND - HALF)) - ROUND
-            high = ((code * (1.0 / 256.0) - (0.5 - 1.0 / 512.0) + ROUND) - ROUND) * 256.0
-            high_ref[at : at + SLAB, lanes] = high.astype(jnp.bfloat16)
-            low_ref[at : at + SLAB, lanes] = (code - high).astype(jnp.bfloat16)
-    parts = [
-        lax.dot_general(
-            pick_ref[...], ref[...], (((1,), (1,)), ((), ())), preferred_element_type=jnp.float32
-        )
-        for ref in (high_ref, low_ref)
-    ]
-    for group in range(BEAMS // 8):
-        rows = slice(8 * group, 8 * group + 8)
-        total = parts[0][rows] + parts[1][rows]
-        both = jnp.concatenate([total[:, : chans // 2], total[:, chans // 2 :]], axis=0)
-        out_ref[group, pl.ds(pl.multiple_of(16 * t, 16), 16), :] = both.astype(jnp.int32).astype(jnp.int16)
-    levels = jnp.transpose(jnp.broadcast_to(level, (chans, 128)))[:1]
-    unit_ref[pl.ds(2 * t, 1), :] = levels[:, : chans // 2]
-    unit_ref[pl.ds(2 * t + 1, 1), :] = levels[:, chans // 2 :]
+        finish()
 
     @pl.when(t == pl.num_programs(1) - 1)
     def _():
@@ -239,10 +229,6 @@
         scratch_shapes=[
             pltpu.VMEM((FEEDS // 128, 2 * block, 128), jnp.float32),
             pltpu.VMEM((8, block // 2), jnp.float32),
-            pltpu.VMEM((block, BEAMS), jnp.float32),
-            pltpu.VMEM((block, 128), jnp.float32),
-            pltpu.VMEM((block, BEAMS), jnp.bfloat16),
-            pltpu.VMEM((block, BEAMS), jnp.bfloat16),
         ],
         compiler_params=pltpu.CompilerParams(vmem_limit_bytes=56 * 2**20),
         cost_estimate=pl.CostEstimate(
@@ -343,10 +329,7 @@
         landed_ref[me] = total_ref[pl.ds(pl.multiple_of(me * rows, 8), rows), :]
         for each in copies:
             each.wait()
-        scale = 1.0 / math.sqrt(CHANNELS)
-        for shard in range(shards):
-            for t in range(rows // 8):
-                out_ref[t, 8 * shard : 8 * shard + 8, :] = landed_ref[shard, 8 * t : 8 * t + 8, :] * scale
+        out_ref[...] = landed_ref[...]
 
 
 def sum_delays(held, lags, trials, before):
@@ -376,13 +359,12 @@
             cost_estimate=cost,
             name="sum_delays",
         )(held, lags, trials)
-    samples = TIME // shards
     return pl.pallas_call(
         share_kernel,
         grid=(subs // TOGETHER,),
         in_specs=in_specs + [whole],
-        out_specs=pl.BlockSpec((samples, 8 * shards, NDM), lambda s: (0, 0, 0)),
-        out_shape=jax.ShapeDtypeStruct((samples, 8 * shards, NDM), jnp.float32),
+        out_specs=pl.BlockSpec((shards, rows // shards, NDM), lambda s: (0, 0, 0)),
+        out_shape=jax.ShapeDtypeStruct((shards, rows // shards, NDM), jnp.float32),
         scratch_shapes=[
             pltpu.VMEM((rows, NDM), jnp.float32),
             pltpu.VMEM((shards, rows // shards, NDM), jnp.float32),
@@ -411,7 +393,9 @@
         formed = form_beams(voltages, feeds, table, first, second, pick, deepest, chunk, chans)
         held = lax.all_to_all(formed, AXES, 0, 0)
         total = sum_delays(held, lags[:, chunk : chunk + 1], trials, total)
-    return total.transpose(1, 0, 2)
+    shards, samples = total.shape[0], voltages.shape[1]
+    parts = total.reshape(shards, samples, 8, NDM).transpose(0, 2, 1, 3)
+    return parts.reshape(shards * 8, samples, NDM) * (1.0 / math.sqrt(CHANNELS))
 
 
 def solution(mesh):

time: 116 us -> 114 us (0.983)
  Pallas kernels: 71.4 us -> 67.7 us
  waiting for transfers between devices: 23.9 us -> 25.7 us
  other arithmetic: 0.6 us -> 2.38 us
  local copies, waits for them, and re-layouts: 2.45 us -> 0.68 us
    pallas_call x2, Pallas kernels: 40.1 us -> 36.4 us  [form_beams(): pl.pallas_call(form_kernel, grid=(steps, samples), in_specs=[pl.BlockSpec...]
    all_to_all x2, waiting for transfers between devices: 23.9 us -> 25.7 us  [per_device(): held = lax.all_to_all(formed, AXES, 0, 0)]
    mul x0 -> x1, other arithmetic: none -> 1.78 us  [per_device(): return parts.reshape(shards * 8, samples, NDM) * (1.0 / math.sqrt(CHANNELS))]
    unnamed x7 -> x6, local copies, waits for them, and re-layouts: 1.78 us -> 0.01 us
  transfers between devices with their start and end apart: 2 -> 2, of which waited for: 2 -> 2; matrix products, arithmetic and copies ran while one was open for 1% -> 1% of each run, Pallas kernels for 26% -> 24%
where the time goes in v4:
time: 114 us
  Pallas kernels  67.7 us (59%)
  waiting for transfers between devices  25.7 us (23%)
  starting transfers between devices  17.5 us (15%)
  other arithmetic  2.38 us (2%)
    pallas_call x2, Pallas kernels, form_beams(): pl.pallas_call(form_kernel, grid=(steps, samples), in_specs=[pl.BlockSpec...  36.4 us
    all_to_all x2, waiting for transfers between devices, per_device(): held = lax.all_to_all(formed, AXES, 0, 0)  25.7 us
    all_to_all x2, starting transfers between devices, per_device(): held = lax.all_to_all(formed, AXES, 0, 0)  17.5 us
    pallas_call x1, Pallas kernels, sum_delays(): pl.pallas_call(share_kernel, grid=(subs // TOGETHER,), in_specs=in_specs...  15.2 us
    pallas_call x1, Pallas kernels, sum_delays(): pl.pallas_call(sum_kernel, grid=(subs // TOGETHER,), in_specs=in_specs, o...  9.65 us
    pallas_call x1, Pallas kernels, route(): pl.pallas_call(route_kernel, in_specs=[whole, whole, whole], out_specs=[w...  6.47 us
  transfers between devices with their start and end apart: 2, of which 2 were waited for; matrix products, arithmetic and copies ran while one was open for 1% of the time, Pallas kernels for 24%

profile of v4, /device:TPU:1, one launch (start us, length us, event | category | flops | bytes accessed | tf_op | source)
XLA Modules:
  0.0 114.0 jit_solution(10700787517712766199)
XLA Ops:
  0.0 6.5 %route.1 = (bf16[8,256,512]{2,1,0:T(8,128)(2,1)}, bf16[8,512,256]{2,1,0:T(8,128)(2,1)}, bf16[1024,1024]{1,0:T(8,128)(2,1)}, s32[1]{0:T(128)}) custom-call(s32[1,2048]{1,0:T(1,128)} %bitcast.10, s32[1,1024]{1,0:T(1,128)} %bitcast.13, bf16[256,256]{1,0:T(8,128)(2,1)} %constant.4.clone.table_ref), custom_call_target="tpu_custom_call" | custom-call | tf_op jit(solution)/shard_map/route/pallas_call | solution.py:85
  6.5 18.3 %form_beams.3 = s16[128,56,128]{2,1,0:T(8,128)(2,1)} custom-call(bf16[512,3,2,2048]{3,2,1,0:T(2,128)(2,1)} %volt_ref.3, s32[1,2048]{1,0:T(1,128)} %bitcast.11, bf16[256,256]{1,0:T(8,128)(2,1)} %constant.4.clone.table_ref, bf16[8,256,512]{2,1,0:T(8,128)(2,1)} %get-tuple-element.9.first_ref, bf16[8,512,256]{2,1,0:T(8,128)(2,1)} %get-tuple-element.10.second_ref, ...), custom_call_target="tpu_custom_call" | custom-call | flops 9663676416 | bytes 12582912 | tf_op jit(solution)/shard_map/form_beams/pallas_call | solution.py:215
  24.8 11.5 %all-to-all-start.1 = ((s16[128,56,128]{2,1,0:T(8,128)(2,1)}), s16[128,56,128]{2,1,0:T(8,128)(2,1)S(1)}, u32[]{:S(2)}, u32[]{:S(2)}) async-start(s16[128,56,128]{2,1,0:T(8,128)(2,1)} %form_beams.3), calls=%async_computation.1 | async-start | bytes 3670016 | tf_op jit(solution)/shard_map/all_to_all | solution.py:394
  36.4 18.1 %form_beams.2 = s16[128,56,128]{2,1,0:T(8,128)(2,1)} custom-call(bf16[512,3,2,2048]{3,2,1,0:T(2,128)(2,1)} %volt_ref.3, s32[1,2048]{1,0:T(1,128)} %bitcast.12, bf16[256,256]{1,0:T(8,128)(2,1)} %constant.4.clone.table_ref, bf16[8,256,512]{2,1,0:T(8,128)(2,1)} %get-tuple-element.9.first_ref, bf16[8,512,256]{2,1,0:T(8,128)(2,1)} %get-tuple-element.10.second_ref, ...), custom_call_target="tpu_custom_call" | custom-call | flops 9663676416 | bytes 12582912 | tf_op jit(solution)/shard_map/form_beams/pallas_call | solution.py:215
  54.5 0.0 copy-start.1
  54.5 0.0 copy-start.2
  54.5 9.4 %all-to-all-done.1.held_ref = s16[128,56,128]{2,1,0:T(8,128)(2,1)S(1)} async-done(((s16[128,56,128]{2,1,0:T(8,128)(2,1)}), s16[128,56,128]{2,1,0:T(8,128)(2,1)S(1)}, u32[]{:S(2)}, u32[]{:S(2)}) %all-to-all-start.1) | async-done | bytes 1835040 | tf_op jit(solution)/shard_map/all_to_all | solution.py:394
  63.8 0.0 copy-start
  63.8 5.9 %all-to-all-start = ((s16[128,56,128]{2,1,0:T(8,128)(2,1)}), s16[128,56,128]{2,1,0:T(8,128)(2,1)}, u32[]{:S(2)}, u32[]{:S(2)}) async-start(s16[128,56,128]{2,1,0:T(8,128)(2,1)} %form_beams.2), calls=%async_computation | async-start | bytes 3670016 | tf_op jit(solution)/shard_map/all_to_all | solution.py:394
  69.8 0.0 copy-done.1
  69.8 0.0 copy-done.2
  69.8 0.6 convert_element_type.7
  70.4 0.6 fusion
  71.1 0.0 copy-done
  71.1 9.7 %sum_delays.1.before_ref = f32[192,512]{1,0:T(8,128)} custom-call(s16[128,56,128]{2,1,0:T(8,128)(2,1)} %copy-done, f32[16,1,256]{2,1,0:T(1,128)} %get-tuple-element.13.lag_ref, f32[1,512]{1,0:T(1,128)} %bitcast.14), custom_call_target="tpu_custom_call" | custom-call | flops 5637144576 | bytes 1572864 | tf_op jit(solution)/shard_map/sum_delays/pallas_call | solution.py:352
  80.7 16.3 %all-to-all-done.held_ref = s16[128,56,128]{2,1,0:T(8,128)(2,1)} async-done(((s16[128,56,128]{2,1,0:T(8,128)(2,1)}), s16[128,56,128]{2,1,0:T(8,128)(2,1)}, u32[]{:S(2)}, u32[]{:S(2)}) %all-to-all-start) | async-done | bytes 1835040 | tf_op jit(solution)/shard_map/all_to_all | solution.py:394
  97.1 15.2 %sum_and_share.1 = f32[8,24,512]{2,1,0:T(8,128)} custom-call(s16[128,56,128]{2,1,0:T(8,128)(2,1)} %all-to-all-done.held_ref, f32[16,1,256]{2,1,0:T(1,128)} %get-tuple-element.14.lag_ref, f32[1,512]{1,0:T(1,128)} %bitcast.15, f32[192,512]{1,0:T(8,128)} %sum_delays.1.before_ref), custom_call_target="tpu_custom_call" | custom-call | flops 5637144576 | bytes 1572864 | tf_op jit(solution)/shard_map/sum_and_share/pallas_call | solution.py:362
  112.3 1.8 %copy_bitcast_fusion = f32[64,3,512]{2,0,1:T(8,128)} fusion(f32[8,24,512]{2,1,0:T(8,128)} %sum_and_share.1), kind=kLoop, calls=%fused_computation | loop fusion | flops 98304 | bytes 786432 | tf_op jit(solution)/shard_map/mul | solution.py:398
  (2 shorter events, 0.0 us)
Async XLA Ops:
  24.8 39.0 %all-to-all-start.1 = ((s16[128,56,128]{2,1,0:T(8,128)(2,1)}), s16[128,56,128]{2,1,0:T(8,128)(2,1)S(1)}, u32[]{:S(2)}, u32[]{:S(2)}) async-start(s16[128,56,128]{2,1,0:T(8,128)(2,1)} %form_beams.3), calls=%async_computation.1 | async-start | bytes 3670016 | tf_op jit(solution)/shard_map/all_to_all | solution.py:394
  54.5 15.3 %copy-start.1 = (s32[8192]{0:T(1024)S(1)}, s32[8192]{0:T(1024)}, u32[]{:S(2)}) copy-start(s32[8192]{0:T(1024)} %param.8) | copy-start | bytes 98308
  54.5 15.4 %copy-start.2 = (s32[512]{0:T(512)S(1)}, s32[512]{0:T(512)}, u32[]{:S(2)}) copy-start(s32[512]{0:T(512)} %param.9) | copy-start | bytes 6148
  63.8 7.3 %copy-start = (s16[128,56,128]{2,1,0:T(8,128)(2,1)}, s16[128,56,128]{2,1,0:T(8,128)(2,1)S(1)}, u32[]{:S(2)}) copy-start(s16[128,56,128]{2,1,0:T(8,128)(2,1)S(1)} %all-to-all-done.1.held_ref) | copy-start | bytes 5505028
  63.8 33.3 %all-to-all-start = ((s16[128,56,128]{2,1,0:T(8,128)(2,1)}), s16[128,56,128]{2,1,0:T(8,128)(2,1)}, u32[]{:S(2)}, u32[]{:S(2)}) async-start(s16[128,56,128]{2,1,0:T(8,128)(2,1)} %form_beams.2), calls=%async_computation | async-start | bytes 3670016 | tf_op jit(solution)/shard_map/all_to_all | solution.py:394

commit v5 on v4

--- a/solution.py
+++ b/solution.py
@@ -98,7 +98,7 @@
 
 
 def form_kernel(
-    volt_ref, feed_ref, table_ref, first_ref, second_ref, pick_ref, deepest_ref, out_ref, grid_ref, unit_ref
+    volt_ref, feed_ref, table_ref, first_ref, second_ref, pick_ref, deepest_ref, out_ref, first_tiles, second_tiles, unit_ref
 ):
     chans = volt_ref.shape[0]
     half = NS // 2
@@ -108,35 +108,35 @@
     def _():
         unit_ref[...] = jnp.zeros_like(unit_ref)
 
-    def finish():
-        edge = lax.broadcasted_iota(jnp.int32, (chans, half), 1) == 0
-
-        def west(p, part):
-            re, im = [], []
-            for y in range(CYL):
-                tile = 2 * (p * CYL + y) + part
-                re.append(grid_ref[tile, pl.ds(0, chans, stride=2), :])
-                im.append(grid_ref[tile, pl.ds(1, chans, stride=2), :])
-            a_re, a_im = re[0] + re[2], im[0] + im[2]
-            b_re, b_im = re[0] - re[2], im[0] - im[2]
-            c_re, c_im = re[1] + re[3], im[1] + im[3]
-            d_re, d_im = re[1] - re[3], im[1] - im[3]
-            return [
-                (a_re + c_re, a_im + c_im),
-                (b_re + d_im, b_im - d_re),
-                (a_re - c_re, a_im - c_im),
-                (b_re - d_im, b_im + d_re),
-            ]
-
-        power = [None] * (2 * CYL)
-        for p in range(POL):
-            for e, ((c_re, c_im), (s_re, s_im)) in enumerate(zip(west(p, 0), west(p, 1))):
-                t_re, t_im = jnp.where(edge, 0.0, s_re), jnp.where(edge, 0.0, s_im)
-                u_re, u_im = c_re + t_im, c_im - t_re
-                v_re, v_im = jnp.where(edge, s_re, c_re - t_im), jnp.where(edge, s_im, c_im + t_re)
-                for at, (w_re, w_im) in ((2 * e, (u_re, u_im)), (2 * e + 1, (v_re, v_im))):
-                    square = w_re * w_re + w_im * w_im
-                    power[at] = square if power[at] is None else power[at] + square
+    edge = lax.broadcasted_iota(jnp.int32, (chans, half), 1) == 0
+
+    def west(tiles_ref, part):
+        re, im = [], []
+        for y in range(CYL):
+            tile = 2 * y + part
+            re.append(tiles_ref[tile, pl.ds(0, chans, stride=2), :])
+            im.append(tiles_ref[tile, pl.ds(1, chans, stride=2), :])
+        a_re, a_im = re[0] + re[2], im[0] + im[2]
+        b_re, b_im = re[0] - re[2], im[0] - im[2]
+        c_re, c_im = re[1] + re[3], im[1] + im[3]
+        d_re, d_im = re[1] - re[3], im[1] - im[3]
+        return [
+            (a_re + c_re, a_im + c_im),
+            (b_re + d_im, b_im - d_re),
+            (a_re - c_re, a_im - c_im),
+            (b_re - d_im, b_im + d_re),
+        ]
+
+    def add_power(power, tiles_ref):
+        for e, ((c_re, c_im), (s_re, s_im)) in enumerate(zip(west(tiles_ref, 0), west(tiles_ref, 1))):
+            t_re, t_im = jnp.where(edge, 0.0, s_re), jnp.where(edge, 0.0, s_im)
+            u_re, u_im = c_re + t_im, c_im - t_re
+            v_re, v_im = jnp.where(edge, s_re, c_re - t_im), jnp.where(edge, s_im, c_im + t_re)
+            for at, (w_re, w_im) in ((2 * e, (u_re, u_im)), (2 * e + 1, (v_re, v_im))):
+                square = w_re * w_re + w_im * w_im
+                power[at] = square if power[at] is None else power[at] + square
+
+    def finish(power):
         power = jnp.concatenate(power, axis=1)
         most = jnp.maximum(jnp.max(power, axis=1, keepdims=True), 1e-30)
         level = jnp.ceil(jnp.log2(most) * STEPS) + 1.0
@@ -157,7 +157,6 @@
         unit_ref[pl.ds(2 * t, 1), :] = levels[:, : chans // 2]
         unit_ref[pl.ds(2 * t + 1, 1), :] = levels[:, chans // 2 :]
 
-
     @pl.when(deepest_ref[0] < ROOM)
     def _():
         rows = volt_ref[:, 0].reshape(2 * chans, FEEDS)
@@ -175,25 +174,33 @@
                 two = ways[1][:, v * half : (v + 1) * half]
                 pieces[2 * v].append(jnp.where(low_half, one, two).astype(jnp.bfloat16))
                 pieces[2 * v + 1].append(jnp.where(low_half, two, one).astype(jnp.bfloat16))
+        power = [None] * (2 * CYL)
+        for p, tiles_ref in enumerate((first_tiles, second_tiles)):
+            for y in range(CYL):
+                d = p * CYL + y
+                wave = jnp.dot(
+                    jnp.concatenate(pieces[d], axis=1), second_ref[d], preferred_element_type=jnp.float32
+                )
+                tiles_ref[2 * y] = wave[:, :half]
+                tiles_ref[2 * y + 1] = wave[:, half:]
+            add_power(power, tiles_ref)
+        finish(power)
+
+    @pl.when(deepest_ref[0] >= ROOM)
+    def _():
+        rows = volt_ref[:, 0].reshape(2 * chans, FEEDS)
+        power = [None] * (2 * CYL)
         for d in range(GROUPS):
-            wave = jnp.dot(
-                jnp.concatenate(pieces[d], axis=1), second_ref[d], preferred_element_type=jnp.float32
-            )
-            grid_ref[2 * d] = wave[:, :half]
-            grid_ref[2 * d + 1] = wave[:, half:]
-        finish()
-
-    @pl.when(deepest_ref[0] >= ROOM)
-    def _():
-        rows = volt_ref[:, 0].reshape(2 * chans, FEEDS)
-        for d in range(GROUPS):
+            tiles_ref, y = (first_tiles, second_tiles)[d // CYL], d % CYL
             feeds = lax.broadcasted_iota(jnp.int32, (FEEDS, NS), 0)
             place = as_onehot(feeds == feed_ref[:, d * NS : (d + 1) * NS])
             slots = jnp.dot(rows, place, preferred_element_type=jnp.float32).astype(jnp.bfloat16)
             wave = jnp.dot(slots, table_ref[...], preferred_element_type=jnp.float32)
-            grid_ref[2 * d] = wave[:, :half]
-            grid_ref[2 * d + 1] = wave[:, half:]
-        finish()
+            tiles_ref[2 * y] = wave[:, :half]
+            tiles_ref[2 * y + 1] = wave[:, half:]
+        add_power(power, first_tiles)
+        add_power(power, second_tiles)
+        finish(power)
 
     @pl.when(t == pl.num_programs(1) - 1)
     def _():
@@ -227,7 +234,8 @@
         out_specs=pl.BlockSpec((groups, ROWS, block // 2), lambda c, t: (0, 0, c)),
         out_shape=jax.ShapeDtypeStruct((groups, ROWS, chans // 2), jnp.int16),
         scratch_shapes=[
-            pltpu.VMEM((FEEDS // 128, 2 * block, 128), jnp.float32),
+            pltpu.VMEM((FEEDS // 256, 2 * block, 128), jnp.float32),
+            pltpu.VMEM((FEEDS // 256, 2 * block, 128), jnp.float32),
             pltpu.VMEM((8, block // 2), jnp.float32),
         ],
         compiler_params=pltpu.CompilerParams(vmem_limit_bytes=56 * 2**20),

time: 114 us -> 114 us (level)
  no operation moved by 1% of the time
where the time goes in v5:
time: 114 us
  Pallas kernels  67.8 us (59%)
  waiting for transfers between devices  25.7 us (23%)
  starting transfers between devices  17.5 us (15%)
  other arithmetic  2.38 us (2%)
    pallas_call x2, Pallas kernels, form_beams(): pl.pallas_call(form_kernel, grid=(steps, samples), in_specs=[pl.BlockSpec...  36.5 us
    all_to_all x2, waiting for transfers between devices, per_device(): held = lax.all_to_all(formed, AXES, 0, 0)  25.7 us
    all_to_all x2, starting transfers between devices, per_device(): held = lax.all_to_all(formed, AXES, 0, 0)  17.5 us
    pallas_call x1, Pallas kernels, sum_delays(): pl.pallas_call(share_kernel, grid=(subs // TOGETHER,), in_specs=in_specs...  15.2 us
    pallas_call x1, Pallas kernels, sum_delays(): pl.pallas_call(sum_kernel, grid=(subs // TOGETHER,), in_specs=in_specs, o...  9.65 us
    pallas_call x1, Pallas kernels, route(): pl.pallas_call(route_kernel, in_specs=[whole, whole, whole], out_specs=[w...  6.47 us
  transfers between devices with their start and end apart: 2, of which 2 were waited for; matrix products, arithmetic and copies ran while one was open for 1% of the time, Pallas kernels for 24%

profile of v5, /device:TPU:1, one launch (start us, length us, event | category | flops | bytes accessed | tf_op | source)
XLA Modules:
  0.0 114.0 jit_solution(5007663779474483380)
XLA Ops:
  0.0 6.5 %route.1 = (bf16[8,256,512]{2,1,0:T(8,128)(2,1)}, bf16[8,512,256]{2,1,0:T(8,128)(2,1)}, bf16[1024,1024]{1,0:T(8,128)(2,1)}, s32[1]{0:T(128)}) custom-call(s32[1,2048]{1,0:T(1,128)} %bitcast.10, s32[1,1024]{1,0:T(1,128)} %bitcast.13, bf16[256,256]{1,0:T(8,128)(2,1)} %constant.4.clone.table_ref), custom_call_target="tpu_custom_call" | custom-call | tf_op jit(solution)/shard_map/route/pallas_call | solution.py:85
  6.5 18.4 %form_beams.3 = s16[128,56,128]{2,1,0:T(8,128)(2,1)} custom-call(bf16[512,3,2,2048]{3,2,1,0:T(2,128)(2,1)} %volt_ref.3, s32[1,2048]{1,0:T(1,128)} %bitcast.11, bf16[256,256]{1,0:T(8,128)(2,1)} %constant.4.clone.table_ref, bf16[8,256,512]{2,1,0:T(8,128)(2,1)} %get-tuple-element.9.first_ref, bf16[8,512,256]{2,1,0:T(8,128)(2,1)} %get-tuple-element.10.second_ref, ...), custom_call_target="tpu_custom_call" | custom-call | flops 9663676416 | bytes 12582912 | tf_op jit(solution)/shard_map/form_beams/pallas_call | solution.py:222
  24.9 11.5 %all-to-all-start.1 = ((s16[128,56,128]{2,1,0:T(8,128)(2,1)}), s16[128,56,128]{2,1,0:T(8,128)(2,1)S(1)}, u32[]{:S(2)}, u32[]{:S(2)}) async-start(s16[128,56,128]{2,1,0:T(8,128)(2,1)} %form_beams.3), calls=%async_computation.1 | async-start | bytes 3670016 | tf_op jit(solution)/shard_map/all_to_all | solution.py:402
  36.4 18.1 %form_beams.2 = s16[128,56,128]{2,1,0:T(8,128)(2,1)} custom-call(bf16[512,3,2,2048]{3,2,1,0:T(2,128)(2,1)} %volt_ref.3, s32[1,2048]{1,0:T(1,128)} %bitcast.12, bf16[256,256]{1,0:T(8,128)(2,1)} %constant.4.clone.table_ref, bf16[8,256,512]{2,1,0:T(8,128)(2,1)} %get-tuple-element.9.first_ref, bf16[8,512,256]{2,1,0:T(8,128)(2,1)} %get-tuple-element.10.second_ref, ...), custom_call_target="tpu_custom_call" | custom-call | flops 9663676416 | bytes 12582912 | tf_op jit(solution)/shard_map/form_beams/pallas_call | solution.py:222
  54.5 0.0 copy-start.1
  54.5 0.0 copy-start.2
  54.5 9.3 %all-to-all-done.1.held_ref = s16[128,56,128]{2,1,0:T(8,128)(2,1)S(1)} async-done(((s16[128,56,128]{2,1,0:T(8,128)(2,1)}), s16[128,56,128]{2,1,0:T(8,128)(2,1)S(1)}, u32[]{:S(2)}, u32[]{:S(2)}) %all-to-all-start.1) | async-done | bytes 1835040 | tf_op jit(solution)/shard_map/all_to_all | solution.py:402
  63.8 0.0 copy-start
  63.8 5.9 %all-to-all-start = ((s16[128,56,128]{2,1,0:T(8,128)(2,1)}), s16[128,56,128]{2,1,0:T(8,128)(2,1)}, u32[]{:S(2)}, u32[]{:S(2)}) async-start(s16[128,56,128]{2,1,0:T(8,128)(2,1)} %form_beams.2), calls=%async_computation | async-start | bytes 3670016 | tf_op jit(solution)/shard_map/all_to_all | solution.py:402
  69.8 0.0 copy-done.1
  69.8 0.0 copy-done.2
  69.8 0.6 convert_element_type.7
  70.4 0.6 fusion
  71.1 0.0 copy-done
  71.1 9.7 %sum_delays.1.before_ref = f32[192,512]{1,0:T(8,128)} custom-call(s16[128,56,128]{2,1,0:T(8,128)(2,1)} %copy-done, f32[16,1,256]{2,1,0:T(1,128)} %get-tuple-element.13.lag_ref, f32[1,512]{1,0:T(1,128)} %bitcast.14), custom_call_target="tpu_custom_call" | custom-call | flops 5637144576 | bytes 1572864 | tf_op jit(solution)/shard_map/sum_delays/pallas_call | solution.py:360
  80.7 16.4 %all-to-all-done.held_ref = s16[128,56,128]{2,1,0:T(8,128)(2,1)} async-done(((s16[128,56,128]{2,1,0:T(8,128)(2,1)}), s16[128,56,128]{2,1,0:T(8,128)(2,1)}, u32[]{:S(2)}, u32[]{:S(2)}) %all-to-all-start) | async-done | bytes 1835040 | tf_op jit(solution)/shard_map/all_to_all | solution.py:402
  97.1 15.2 %sum_and_share.1 = f32[8,24,512]{2,1,0:T(8,128)} custom-call(s16[128,56,128]{2,1,0:T(8,128)(2,1)} %all-to-all-done.held_ref, f32[16,1,256]{2,1,0:T(1,128)} %get-tuple-element.14.lag_ref, f32[1,512]{1,0:T(1,128)} %bitcast.15, f32[192,512]{1,0:T(8,128)} %sum_delays.1.before_ref), custom_call_target="tpu_custom_call" | custom-call | flops 5637144576 | bytes 1572864 | tf_op jit(solution)/shard_map/sum_and_share/pallas_call | solution.py:370
  112.3 1.8 %copy_bitcast_fusion = f32[64,3,512]{2,0,1:T(8,128)} fusion(f32[8,24,512]{2,1,0:T(8,128)} %sum_and_share.1), kind=kLoop, calls=%fused_computation | loop fusion | flops 98304 | bytes 786432 | tf_op jit(solution)/shard_map/mul | solution.py:406
  (2 shorter events, 0.0 us)
Async XLA Ops:
  24.9 39.0 %all-to-all-start.1 = ((s16[128,56,128]{2,1,0:T(8,128)(2,1)}), s16[128,56,128]{2,1,0:T(8,128)(2,1)S(1)}, u32[]{:S(2)}, u32[]{:S(2)}) async-start(s16[128,56,128]{2,1,0:T(8,128)(2,1)} %form_beams.3), calls=%async_computation.1 | async-start | bytes 3670016 | tf_op jit(solution)/shard_map/all_to_all | solution.py:402
  54.5 15.3 %copy-start.1 = (s32[8192]{0:T(1024)S(1)}, s32[8192]{0:T(1024)}, u32[]{:S(2)}) copy-start(s32[8192]{0:T(1024)} %param.8) | copy-start | bytes 98308
  54.5 15.3 %copy-start.2 = (s32[512]{0:T(512)S(1)}, s32[512]{0:T(512)}, u32[]{:S(2)}) copy-start(s32[512]{0:T(512)} %param.9) | copy-start | bytes 6148
  63.8 7.3 %copy-start = (s16[128,56,128]{2,1,0:T(8,128)(2,1)}, s16[128,56,128]{2,1,0:T(8,128)(2,1)S(1)}, u32[]{:S(2)}) copy-start(s16[128,56,128]{2,1,0:T(8,128)(2,1)S(1)} %all-to-all-done.1.held_ref) | copy-start | bytes 5505028
  63.8 33.3 %all-to-all-start = ((s16[128,56,128]{2,1,0:T(8,128)(2,1)}), s16[128,56,128]{2,1,0:T(8,128)(2,1)}, u32[]{:S(2)}, u32[]{:S(2)}) async-start(s16[128,56,128]{2,1,0:T(8,128)(2,1)} %form_beams.2), calls=%async_computation | async-start | bytes 3670016 | tf_op jit(solution)/shard_map/all_to_all | solution.py:402

commit v6 on v5

--- a/solution.py
+++ b/solution.py
@@ -68,12 +68,20 @@
         second_ref[d] = jnp.dot(
             as_onehot(hit), table_ref[...], preferred_element_type=jnp.float32
         ).astype(jnp.bfloat16)
-    code = jnp.concatenate(codes, axis=1).astype(jnp.float32)
+    code = jnp.concatenate(codes, axis=1)
+    within = as_onehot(lax.broadcasted_iota(jnp.int32, (NS, FEEDS), 0) == feed_ref[...] % NS)
+    mine = lax.broadcasted_iota(jnp.int32, (GROUPS, FEEDS), 0) == feed_ref[...] // NS
+    digits = [jnp.where(mine, digit, 0).astype(jnp.float32) for digit in (code // 16 * 16, code % 16)]
+    columns = lax.dot_general(
+        within,
+        jnp.concatenate(digits, axis=0).astype(jnp.bfloat16),
+        (((1,), (1,)), ((), ())),
+        preferred_element_type=jnp.float32,
+    ).astype(jnp.int32)
+    lanes = lax.broadcasted_iota(jnp.int32, (NS, GROUPS * ROOM), 1)
     for b in range(GROUPS):
-        feeds = lax.broadcasted_iota(jnp.int32, (NS, FEEDS), 0) + b * NS
-        mine = jnp.sum(jnp.where(feeds == feed_ref[...], code, 0.0), axis=1, keepdims=True)
-        lanes = lax.broadcasted_iota(jnp.int32, (NS, GROUPS * ROOM), 1)
-        first_ref[b] = as_onehot(mine.astype(jnp.int32) == lanes)
+        column = columns[:, b : b + 1] + columns[:, GROUPS + b : GROUPS + b + 1]
+        first_ref[b] = as_onehot(column == lanes)
     north = order_ref[...] % NS
     wanted = order_ref[...] - north + jnp.where(north <= NS // 2, north, NS + NS // 2 - north)
     pick_ref[...] = as_onehot(column_of(wanted) == lax.broadcasted_iota(jnp.int32, (BEAMS, BEAMS), 1))

time: 114 us -> 114 us (level)
  no operation moved by 1% of the time
where the time goes in v6:
time: 114 us; the launch traced here: 113 us
  Pallas kernels  67.2 us (59%)
  waiting for transfers between devices  25.7 us (23%)
  starting transfers between devices  17.4 us (15%)
  other arithmetic  2.38 us (2%)
    pallas_call x2, Pallas kernels, form_beams(): pl.pallas_call(form_kernel, grid=(steps, samples), in_specs=[pl.BlockSpec...  36.5 us
    all_to_all x2, waiting for transfers between devices, per_device(): held = lax.all_to_all(formed, AXES, 0, 0)  25.7 us
    all_to_all x2, starting transfers between devices, per_device(): held = lax.all_to_all(formed, AXES, 0, 0)  17.4 us
    pallas_call x1, Pallas kernels, sum_delays(): pl.pallas_call(share_kernel, grid=(subs // TOGETHER,), in_specs=in_specs...  15.2 us
    pallas_call x1, Pallas kernels, sum_delays(): pl.pallas_call(sum_kernel, grid=(subs // TOGETHER,), in_specs=in_specs, o...  9.65 us
    pallas_call x1, Pallas kernels, route(): pl.pallas_call(route_kernel, in_specs=[whole, whole, whole], out_specs=[w...  5.85 us
  transfers between devices with their start and end apart: 2, of which 2 were waited for; matrix products, arithmetic and copies ran while one was open for 1% of the time, Pallas kernels for 24%

profile of v6, /device:TPU:1, one launch (start us, length us, event | category | flops | bytes accessed | tf_op | source)
XLA Modules:
  0.0 113.4 jit_solution(4053735988732951090)
XLA Ops:
  0.0 5.9 %route.1 = (bf16[8,256,512]{2,1,0:T(8,128)(2,1)}, bf16[8,512,256]{2,1,0:T(8,128)(2,1)}, bf16[1024,1024]{1,0:T(8,128)(2,1)}, s32[1]{0:T(128)}) custom-call(s32[1,2048]{1,0:T(1,128)} %bitcast.10, s32[1,1024]{1,0:T(1,128)} %bitcast.13, bf16[256,256]{1,0:T(8,128)(2,1)} %constant.4.clone.table_ref), custom_call_target="tpu_custom_call" | custom-call | tf_op jit(solution)/shard_map/route/pallas_call | solution.py:93
  5.9 18.4 %form_beams.3 = s16[128,56,128]{2,1,0:T(8,128)(2,1)} custom-call(bf16[512,3,2,2048]{3,2,1,0:T(2,128)(2,1)} %volt_ref.3, s32[1,2048]{1,0:T(1,128)} %bitcast.11, bf16[256,256]{1,0:T(8,128)(2,1)} %constant.4.clone.table_ref, bf16[8,256,512]{2,1,0:T(8,128)(2,1)} %get-tuple-element.9.first_ref, bf16[8,512,256]{2,1,0:T(8,128)(2,1)} %get-tuple-element.10.second_ref, ...), custom_call_target="tpu_custom_call" | custom-call | flops 9663676416 | bytes 12582912 | tf_op jit(solution)/shard_map/form_beams/pallas_call | solution.py:230
  24.2 11.5 %all-to-all-start.1 = ((s16[128,56,128]{2,1,0:T(8,128)(2,1)}), s16[128,56,128]{2,1,0:T(8,128)(2,1)S(1)}, u32[]{:S(2)}, u32[]{:S(2)}) async-start(s16[128,56,128]{2,1,0:T(8,128)(2,1)} %form_beams.3), calls=%async_computation.1 | async-start | bytes 3670016 | tf_op jit(solution)/shard_map/all_to_all | solution.py:410
  35.7 18.1 %form_beams.2 = s16[128,56,128]{2,1,0:T(8,128)(2,1)} custom-call(bf16[512,3,2,2048]{3,2,1,0:T(2,128)(2,1)} %volt_ref.3, s32[1,2048]{1,0:T(1,128)} %bitcast.12, bf16[256,256]{1,0:T(8,128)(2,1)} %constant.4.clone.table_ref, bf16[8,256,512]{2,1,0:T(8,128)(2,1)} %get-tuple-element.9.first_ref, bf16[8,512,256]{2,1,0:T(8,128)(2,1)} %get-tuple-element.10.second_ref, ...), custom_call_target="tpu_custom_call" | custom-call | flops 9663676416 | bytes 12582912 | tf_op jit(solution)/shard_map/form_beams/pallas_call | solution.py:230
  53.9 0.0 copy-start.1
  53.9 0.0 copy-start.2
  53.9 9.3 %all-to-all-done.1.held_ref = s16[128,56,128]{2,1,0:T(8,128)(2,1)S(1)} async-done(((s16[128,56,128]{2,1,0:T(8,128)(2,1)}), s16[128,56,128]{2,1,0:T(8,128)(2,1)S(1)}, u32[]{:S(2)}, u32[]{:S(2)}) %all-to-all-start.1) | async-done | bytes 1835040 | tf_op jit(solution)/shard_map/all_to_all | solution.py:410
  63.2 0.0 copy-start
  63.2 5.9 %all-to-all-start = ((s16[128,56,128]{2,1,0:T(8,128)(2,1)}), s16[128,56,128]{2,1,0:T(8,128)(2,1)}, u32[]{:S(2)}, u32[]{:S(2)}) async-start(s16[128,56,128]{2,1,0:T(8,128)(2,1)} %form_beams.2), calls=%async_computation | async-start | bytes 3670016 | tf_op jit(solution)/shard_map/all_to_all | solution.py:410
  69.2 0.0 copy-done.1
  69.2 0.0 copy-done.2
  69.2 0.6 convert_element_type.7
  69.8 0.6 fusion
  70.5 0.0 copy-done
  70.5 9.6 %sum_delays.1.before_ref = f32[192,512]{1,0:T(8,128)} custom-call(s16[128,56,128]{2,1,0:T(8,128)(2,1)} %copy-done, f32[16,1,256]{2,1,0:T(1,128)} %get-tuple-element.13.lag_ref, f32[1,512]{1,0:T(1,128)} %bitcast.14), custom_call_target="tpu_custom_call" | custom-call | flops 5637144576 | bytes 1572864 | tf_op jit(solution)/shard_map/sum_delays/pallas_call | solution.py:368
  80.1 16.4 %all-to-all-done.held_ref = s16[128,56,128]{2,1,0:T(8,128)(2,1)} async-done(((s16[128,56,128]{2,1,0:T(8,128)(2,1)}), s16[128,56,128]{2,1,0:T(8,128)(2,1)}, u32[]{:S(2)}, u32[]{:S(2)}) %all-to-all-start) | async-done | bytes 1835040 | tf_op jit(solution)/shard_map/all_to_all | solution.py:410
  96.5 15.2 %sum_and_share.1 = f32[8,24,512]{2,1,0:T(8,128)} custom-call(s16[128,56,128]{2,1,0:T(8,128)(2,1)} %all-to-all-done.held_ref, f32[16,1,256]{2,1,0:T(1,128)} %get-tuple-element.14.lag_ref, f32[1,512]{1,0:T(1,128)} %bitcast.15, f32[192,512]{1,0:T(8,128)} %sum_delays.1.before_ref), custom_call_target="tpu_custom_call" | custom-call | flops 5637144576 | bytes 1572864 | tf_op jit(solution)/shard_map/sum_and_share/pallas_call | solution.py:378
  111.6 1.8 %copy_bitcast_fusion = f32[64,3,512]{2,0,1:T(8,128)} fusion(f32[8,24,512]{2,1,0:T(8,128)} %sum_and_share.1), kind=kLoop, calls=%fused_computation | loop fusion | flops 98304 | bytes 786432 | tf_op jit(solution)/shard_map/mul | solution.py:414
  (2 shorter events, 0.0 us)
Async XLA Ops:
  24.2 39.0 %all-to-all-start.1 = ((s16[128,56,128]{2,1,0:T(8,128)(2,1)}), s16[128,56,128]{2,1,0:T(8,128)(2,1)S(1)}, u32[]{:S(2)}, u32[]{:S(2)}) async-start(s16[128,56,128]{2,1,0:T(8,128)(2,1)} %form_beams.3), calls=%async_computation.1 | async-start | bytes 3670016 | tf_op jit(solution)/shard_map/all_to_all | solution.py:410
  53.9 15.3 %copy-start.1 = (s32[8192]{0:T(1024)S(1)}, s32[8192]{0:T(1024)}, u32[]{:S(2)}) copy-start(s32[8192]{0:T(1024)} %param.8) | copy-start | bytes 98308
  53.9 15.3 %copy-start.2 = (s32[512]{0:T(512)S(1)}, s32[512]{0:T(512)}, u32[]{:S(2)}) copy-start(s32[512]{0:T(512)} %param.9) | copy-start | bytes 6148
  63.2 7.3 %copy-start = (s16[128,56,128]{2,1,0:T(8,128)(2,1)}, s16[128,56,128]{2,1,0:T(8,128)(2,1)S(1)}, u32[]{:S(2)}) copy-start(s16[128,56,128]{2,1,0:T(8,128)(2,1)S(1)} %all-to-all-done.1.held_ref) | copy-start | bytes 5505028
  63.2 33.3 %all-to-all-start = ((s16[128,56,128]{2,1,0:T(8,128)(2,1)}), s16[128,56,128]{2,1,0:T(8,128)(2,1)}, u32[]{:S(2)}, u32[]{:S(2)}) async-start(s16[128,56,128]{2,1,0:T(8,128)(2,1)} %form_beams.2), calls=%async_computation | async-start | bytes 3670016 | tf_op jit(solution)/shard_map/all_to_all | solution.py:410
